TPU v7x, 32 devices: a whole 2x2x4 slice. The times are simulated.
32 devices in a mesh: row: 4 (over y, x), col: 8 (over z, core).
Axes of the slice: x: 2, y: 2, z: 4, core: 2. Of those that a mesh axis runs over, the one named last changes fastest.
Arguments:
- probe_block: bfloat16 [64, 32768], P(None, ('row', 'col'))
- prior_blocks: bfloat16 [4, 64, 32768], P(None, None, ('row', 'col'))
- self_relatedness: float32 [32768], P(('row', 'col')), may hold values from 0.5 to 2
- tile_values: bfloat16 [160, 1024, 1024], P(('row', 'col')), may hold values from -0.125 to 0.125
- tile_index: int32 [160, 3], P(('row', 'col')), may hold values from 0 to 31, as said below
Outputs:
- residual_block: float32 [64, 32768], P(None, ('row', 'col'))
- coefficients: float32 [5, 64, 64], replicated
Inputs may be any that keep to these rules, and one draw needn't show every extreme that they name: `tile_index`: rows d * 5 to d * 5 + 4 belong to the device d = r * C + c at mesh position (r, c), C the size of the col axis. In a row with column 2 equal to 1 (live) the tile row lies in [r * C, r * C + C), the tile column j has j % C == c, and tile row <= tile column; live pairs of one device are distinct. Column 2 is 0 in dead rows, which repeat the indices of the device's first row. Live counts vary between devices (not all equal), and some device has all 5 rows live.
All inputs are finite; a program needn't handle non-finite values.
Results may differ from a plain program's by a relative error of at most 0.0003.
Values may be sent and summed in bfloat16 or wider, within the bound.
A program may use at most 128 MiB of HBM per device.

v0:
```python
import jax
import jax.numpy as jnp
from jax import lax
from jax.sharding import PartitionSpec as P


def add_span(running, addend, offset):
    current = lax.dynamic_slice_in_dim(running, offset, addend.shape[1], 1)
    return lax.dynamic_update_slice_in_dim(running, current + addend, offset, 1)


def keep_same(partials):
    return partials


def tile_products(tile_values, tile_index, row_probes, col_probes, col_count):
    tile_width = tile_values.shape[1]
    depth = row_probes.shape[0]
    partials = []
    partials.append(jnp.zeros((depth, row_probes.shape[1]), jnp.float32))
    partials.append(jnp.zeros((depth, col_probes.shape[1]), jnp.float32))
    partials = tuple(partials)
    for slot_index in range(tile_values.shape[0]):
        current_tile = tile_values[slot_index]
        row_start = tile_index[slot_index, 0] % col_count * tile_width
        col_start = tile_index[slot_index, 1] // col_count * tile_width

        def apply(state, current_tile=current_tile, row_start=row_start, col_start=col_start):
            updated = list(state)
            position = 0
            right = lax.dynamic_slice_in_dim(col_probes, col_start, tile_width, 1)
            forward = lax.dot_general(
                right, current_tile, (((1,), (1,)), ((), ())), preferred_element_type=jnp.float32
            )
            updated[0] = add_span(updated[0], forward, row_start)
            position = 1
            left = lax.dynamic_slice_in_dim(row_probes, row_start, tile_width, 1)
            mirror = jnp.dot(left, current_tile, preferred_element_type=jnp.float32)
            updated[position] = add_span(updated[position], mirror, col_start)
            return tuple(updated)

        partials = lax.cond(tile_index[slot_index, 2] > 0, apply, keep_same, partials)
    return partials


def sum_rows(row_part):
    return lax.psum_scatter(row_part, "col", scatter_dimension=1, tiled=True)


def sum_columns(col_part):
    return lax.psum_scatter(col_part, "row", scatter_dimension=1, tiled=True)


def solve_block(gram_block, target):
    factor = jnp.linalg.cholesky(gram_block)
    return jax.scipy.linalg.cho_solve((factor, True), target)


def shards(probe_block, prior_blocks, self_relatedness, tile_values, tile_index):
    col_count = lax.axis_size("col")
    block_count = prior_blocks.shape[0] + 1
    basis = jnp.concatenate([prior_blocks, probe_block[None]], axis=0)
    row_probes = lax.all_gather(probe_block, "col", axis=1, tiled=True)
    col_probes = lax.all_gather(probe_block, "row", axis=1, tiled=True)
    row_part, col_part = tile_products(tile_values, tile_index, row_probes, col_probes, col_count)
    row_total = sum_rows(row_part)
    col_total = sum_columns(col_part)
    product = self_relatedness[None, :] * probe_block.astype(jnp.float32) + row_total + col_total
    current = product
    solved = []
    for block_number in range(block_count):
        basis_block = basis[block_number]
        wide_block = basis_block.astype(jnp.float32)
        gram_local = jnp.dot(basis_block, basis_block.T, preferred_element_type=jnp.float32)
        along_local = jnp.dot(wide_block, current.T, precision=lax.Precision.HIGHEST)
        gram_block, along = lax.psum((gram_local, along_local), ("row", "col"))
        coefficient = solve_block(gram_block, along)
        solved.append(coefficient)
        current = current - jnp.dot(coefficient.T, wide_block, precision=lax.Precision.HIGHEST)
    return (current, jnp.stack(solved))


def solution(mesh):
    in_specs = (
        P(None, ("row", "col")),
        P(None, None, ("row", "col")),
        P(("row", "col")),
        P(("row", "col"), None, None),
        P(("row", "col"), None),
    )
    out_specs = (P(None, ("row", "col")), P())
    return jax.shard_map(shards, mesh=mesh, in_specs=in_specs, out_specs=out_specs, check_vma=False)
```

profile of v0, /device:TPU:0, one launch (start us, length us, event | category | flops | bytes accessed | tf_op | source)
XLA Modules:
  0.0 436.5 jit_solution(12915981944628994449)
XLA Ops:
  7.9 1.9 fusion.98
  30.8 11.8 %all_gather.6 = bf16[64,4096]{1,0:T(8,128)(2,1)S(1)} all-gather(bf16[64,1024]{1,0:T(8,128)(2,1)} %param.18), channel_id=1, replica_groups=mesh['row'=4,'col'=8] {'row'}, dimensions={1}, use_global_device_ids=true | all-gather | bytes 655360 | tf_op jit(solution)/shard_map/all_gather | solution.py:64
  42.7 5.7 %slice_bitcast_fusion = (bf16[1024,1024]{1,0:T(8,128)(2,1)S(1)}, bf16[1024,1024]{1,0:T(8,128)(2,1)}, bf16[1024,1024]{1,0:T(8,128)(2,1)}, bf16[1024,1024]{1,0:T(8,128)(2,1)}) fusion(bf16[5,1024,1024]{2,1,0:T(8,128)(2,1)} %param.21), kind=kLoop, calls=%fused_computation.38 | loop fusion | bytes 16777216 | tf_op jit(solution)/shard_map/squeeze | solution.py:24
  48.4 10.7 %conditional.5 = (f32[64,8192]{1,0:T(8,128)}, f32[64,4096]{1,0:T(8,128)}) conditional(s32[]{:T(128)} %bitcast.6, () %tuple.49, (s32[]{:T(128)}, bf16[64,4096]{1,0:T(8,128)(2,1)S(1)}, bf16[1024,1024]{1,0:T(8,128)(2,1)}, s32[]{:T(128)}, bf16[64,8192]{1,0:T(8,128)(2,1)}) %tuple.50), branch_computations={%region_0.1_spmd, %region_1.2_spmd} | conditional | flops 268435456 | bytes 9175148 | solution.py:42
  48.4 2.3 fusion.2
  52.2 1.8 dynamic_update_slice.26
  54.0 2.2 fusion
  59.1 8.1 %conditional.6 = ((f32[64,8192]{1,0:T(8,128)}, f32[64,4096]{1,0:T(8,128)})) conditional(s32[]{:T(128)} %bitcast.5, (f32[64,8192]{1,0:T(8,128)}, f32[64,4096]{1,0:T(8,128)}) %conditional.5, (s32[]{:T(128)}, f32[64,8192]{1,0:T(8,128)}, s32[]{:T(128)}, bf16[64,4096]{1,0:T(8,128)(2,1)S(1)}, bf16[1024,1024]{1,0:T(8,128)(2,1)}, ...), branch_computations={%region_2.3_spmd, %region_3.4_spmd} | conditional | flops 268566528 | bytes 6553716 | solution.py:42
  59.1 2.4 convolution_add_fusion.1
  63.1 2.2 convolution_add_fusion
  65.3 1.8 dynamic_update_slice.29
  67.1 8.1 %conditional.7 = ((f32[64,8192]{1,0:T(8,128)}, f32[64,4096]{1,0:T(8,128)})) conditional(s32[]{:T(128)} %bitcast.4, (f32[64,8192]{1,0:T(8,128)}, f32[64,4096]{1,0:T(8,128)}) %get-tuple-element.388, (s32[]{:T(128)}, f32[64,8192]{1,0:T(8,128)}, s32[]{:T(128)}, bf16[64,4096]{1,0:T(8,128)(2,1)S(1)}, bf16[1024,1024]{1,0:T(8,128)(2,1)}, ...), branch_computations={%region_4.5_spmd, %region_5.6_spmd} | conditional | flops 268566528 | bytes 6553716 | solution.py:42
  67.1 2.4 convolution_add_fusion.3
  69.5 1.8 dynamic_update_slice.30
  71.3 2.2 convolution_add_fusion.2
  77.2 44.4 %reduce-scatter.5.cloned.1.call-done = f32[64,1024]{1,0:T(8,128)} async-done(((f32[64,4096]{1,0:T(8,128)}), f32[64,1024]{1,0:T(8,128)}) %reduce-scatter.5.cloned.1.call-update) | async-done | bytes 262160 | tf_op jit(solution)/shard_map/reduce_scatter | solution.py:51
  121.5 38.2 %reduce-scatter.3.cloned.1.call-done = f32[64,1024]{1,0:T(8,128)} async-done(((f32[64,8192]{1,0:T(8,128)}), f32[64,1024]{1,0:T(8,128)}) %reduce-scatter.3.cloned.1.call-update) | async-done | bytes 262160 | tf_op jit(solution)/shard_map/reduce_scatter | solution.py:47
  161.0 38.4 %all-reduce.4 = (f32[64,64]{0,1:T(8,128)S(1)}, f32[64,64]{0,1:T(8,128)S(1)}) all-reduce(f32[64,64]{0,1:T(8,128)S(1)} %convolution_bitcast_fusion.4, f32[64,64]{0,1:T(8,128)S(1)} %fusion.54), channel_id=1, replica_groups=mesh['row'=4,'col'=8] {'row','col'}, use_global_device_ids=true, to_apply=%region_15.17 | all-reduce | flops 8192 | bytes 65536 | tf_op jit(solution)/shard_map/psum | solution.py:76
  199.5 5.8 %cholesky.89 = f32[64,64]{1,0:T(8,128)S(1)} custom-call(f32[64,64]{1,0:T(8,128)S(1)} %fusion.97), custom_call_target="Cholesky" | custom-call | tf_op jit(solution)/shard_map/jit(cholesky)/cholesky | solution.py:55
  206.7 4.9 %custom-call.11 = f32[1,64,64]{1,2,0:T(8,128)S(1)} custom-call(f32[1,64,64]{2,1,0:T(8,128)S(1)} %fusion.68), custom_call_target="InvertDiagBlocksLowerTriangular" | custom-call | tf_op jit(solution)/shard_map/jit(_cho_solve)/triangular_solve | solution.py:56
  213.6 42.1 %all-reduce.3 = (f32[64,64]{0,1:T(8,128)S(1)}, f32[64,64]{0,1:T(8,128)S(1)}) all-reduce(f32[64,64]{0,1:T(8,128)S(1)} %convolution_bitcast_fusion.3, f32[64,64]{0,1:T(8,128)S(1)} %fusion.50), channel_id=1, replica_groups=mesh['row'=4,'col'=8] {'row','col'}, use_global_device_ids=true, to_apply=%region_17.20 | all-reduce | flops 8192 | bytes 65536 | tf_op jit(solution)/shard_map/psum | solution.py:76
  255.9 5.8 %cholesky.100 = f32[64,64]{1,0:T(8,128)S(1)} custom-call(f32[64,64]{1,0:T(8,128)S(1)} %fusion.92), custom_call_target="Cholesky" | custom-call | tf_op jit(solution)/shard_map/jit(cholesky)/cholesky | solution.py:55
  263.0 4.9 %custom-call.12 = f32[1,64,64]{1,2,0:T(8,128)S(1)} custom-call(f32[1,64,64]{2,1,0:T(8,128)S(1)} %fusion.69), custom_call_target="InvertDiagBlocksLowerTriangular" | custom-call | tf_op jit(solution)/shard_map/jit(_cho_solve)/triangular_solve | solution.py:56
  268.9 39.8 %all-reduce.2 = (f32[64,64]{0,1:T(8,128)S(1)}, f32[64,64]{0,1:T(8,128)S(1)}) all-reduce(f32[64,64]{0,1:T(8,128)S(1)} %convolution_bitcast_fusion.2, f32[64,64]{0,1:T(8,128)S(1)} %fusion.46), channel_id=1, replica_groups=mesh['row'=4,'col'=8] {'row','col'}, use_global_device_ids=true, to_apply=%region_19.22 | all-reduce | flops 8192 | bytes 65536 | tf_op jit(solution)/shard_map/psum | solution.py:76
  308.9 5.8 %cholesky.111 = f32[64,64]{1,0:T(8,128)S(1)} custom-call(f32[64,64]{1,0:T(8,128)S(1)} %fusion.87), custom_call_target="Cholesky" | custom-call | tf_op jit(solution)/shard_map/jit(cholesky)/cholesky | solution.py:55
  316.1 4.9 %custom-call.13 = f32[1,64,64]{1,2,0:T(8,128)S(1)} custom-call(f32[1,64,64]{2,1,0:T(8,128)S(1)} %fusion.70), custom_call_target="InvertDiagBlocksLowerTriangular" | custom-call | tf_op jit(solution)/shard_map/jit(_cho_solve)/triangular_solve | solution.py:56
  322.0 41.2 %all-reduce.1 = (f32[64,64]{0,1:T(8,128)S(1)}, f32[64,64]{0,1:T(8,128)S(1)}) all-reduce(f32[64,64]{0,1:T(8,128)S(1)} %convolution_bitcast_fusion.1, f32[64,64]{0,1:T(8,128)S(1)} %fusion.42), channel_id=1, replica_groups=mesh['row'=4,'col'=8] {'row','col'}, use_global_device_ids=true, to_apply=%region_21.24 | all-reduce | flops 8192 | bytes 65536 | tf_op jit(solution)/shard_map/psum | solution.py:76
  363.2 5.8 %cholesky.122 = f32[64,64]{1,0:T(8,128)S(1)} custom-call(f32[64,64]{1,0:T(8,128)S(1)} %fusion.82), custom_call_target="Cholesky" | custom-call | tf_op jit(solution)/shard_map/jit(cholesky)/cholesky | solution.py:55
  370.4 4.9 %custom-call.14 = f32[1,64,64]{1,2,0:T(8,128)S(1)} custom-call(f32[1,64,64]{2,1,0:T(8,128)S(1)} %fusion.71), custom_call_target="InvertDiagBlocksLowerTriangular" | custom-call | tf_op jit(solution)/shard_map/jit(_cho_solve)/triangular_solve | solution.py:56
  376.3 40.1 %all-reduce = (f32[64,64]{0,1:T(8,128)S(1)}, f32[64,64]{0,1:T(8,128)S(1)}) all-reduce(f32[64,64]{0,1:T(8,128)S(1)} %convolution_bitcast_fusion, f32[64,64]{0,1:T(8,128)S(1)} %fusion.99), channel_id=1, replica_groups=mesh['row'=4,'col'=8] {'row','col'}, use_global_device_ids=true, to_apply=%region_23.26 | all-reduce | flops 8192 | bytes 65536 | tf_op jit(solution)/shard_map/psum | solution.py:76
  416.5 5.8 %cholesky.133 = f32[64,64]{1,0:T(8,128)S(1)} custom-call(f32[64,64]{1,0:T(8,128)S(1)} %fusion.77), custom_call_target="Cholesky" | custom-call | tf_op jit(solution)/shard_map/jit(cholesky)/cholesky | solution.py:55
  423.7 4.9 %custom-call.15 = f32[1,64,64]{1,2,0:T(8,128)S(1)} custom-call(f32[1,64,64]{2,1,0:T(8,128)S(1)} %fusion.72), custom_call_target="InvertDiagBlocksLowerTriangular" | custom-call | tf_op jit(solution)/shard_map/jit(_cho_solve)/triangular_solve | solution.py:56
  (72 shorter events, 25.1 us)
Async XLA Ops:
  7.2 41.2 %all-gather.2.cloned.1.call-start = ((), (), s32[]{:S(2)}) async-start(), calls=%async_computation.2 | async-start | bytes 1179648 | tf_op jit(solution)/shard_map/all_gather | solution.py:63
  7.9 113.6 %reduce-scatter.5.cloned.1.call-start = ((), (), s32[]{:S(2)}) async-start(), calls=%async_computation.4 | async-start | bytes 1310720 | tf_op jit(solution)/shard_map/reduce_scatter | solution.py:51
  75.2 1.0 copy-start.1
  75.2 1.8 copy-start
  75.2 84.5 %copy-start.2 = (f32[1024]{0:T(1024)S(1)}, f32[1024]{0:T(1024)}, u32[]{:S(2)}) copy-start(f32[1024]{0:T(1024)} %param.20) | copy-start | bytes 12292
  75.3 84.5 %reduce-scatter.3.cloned.1.call-start = ((), (), s32[]{:S(2)}) async-start(), calls=%async_computation.3 | async-start | bytes 2359296 | tf_op jit(solution)/shard_map/reduce_scatter | solution.py:47
  429.0 1.0 copy-start.3
Sparse Core Ops, SparseCore 0:
  9.6 24.8 all-gather.1
  75.4 46.0 reduce-scatter.4
  123.9 35.7 reduce-scatter.2
where the time goes:
time: 437 us
  blocking collectives  213 us (49%)
  waiting for transfers between devices  83.9 us (19%)
  other arithmetic  60.4 us (14%)
  between operations  35.1 us (8%)
  matrix products  22.2 us (5%)
  local copies, waits for them, and re-layouts  21.4 us (5%)
    psum x5, blocking collectives, shards(): gram_block, along = lax.psum((gram_local, along_local), ('row', 'col'))  202 us
    reduce_scatter x1, waiting for transfers between devices, sum_columns(): return lax.psum_scatter(col_part, 'row', scatter_dimension=1, tiled=True)  44.4 us
    reduce_scatter x1, waiting for transfers between devices, sum_rows(): return lax.psum_scatter(row_part, 'col', scatter_dimension=1, tiled=True)  38.2 us
    another operation x15, other arithmetic, solve_block(): factor = jnp.linalg.cholesky(gram_block)  32.6 us
    another operation x10, other arithmetic, solve_block(): return jax.scipy.linalg.cho_solve((factor, True), target)  27.7 us
    all_gather x1, blocking collectives, shards(): col_probes = lax.all_gather(probe_block, 'row', axis=1, tiled=True)  11.8 us
    dynamic_update_slice x6, local copies, waits for them, and re-layouts, add_span(): return lax.dynamic_update_slice_in_dim(running, current + addend, offset, 1)  10.6 us
  transfers between devices with their start and end apart: 3, of which 2 were waited for; matrix products, arithmetic and copies ran while one was open for 2% of the time, Pallas kernels for 0%

commit v1 on v0

v1 whole, which is shorter than its diff:
```python
import jax
import jax.numpy as jnp
from jax import lax
from jax.sharding import PartitionSpec as P

HIGH = lax.Precision.HIGHEST


def add_span(running, addend, offset):
    current = lax.dynamic_slice_in_dim(running, offset, addend.shape[1], 1)
    return lax.dynamic_update_slice_in_dim(running, current + addend, offset, 1)


def keep_same(partials):
    return partials


def tile_products(tile_values, tile_index, row_probes, col_probes, col_count):
    tile_width = tile_values.shape[1]
    depth = row_probes.shape[0]
    partials = (
        jnp.zeros((depth, row_probes.shape[1]), jnp.float32),
        jnp.zeros((depth, col_probes.shape[1]), jnp.float32),
    )
    for slot_index in range(tile_values.shape[0]):
        current_tile = tile_values[slot_index]
        row_start = tile_index[slot_index, 0] % col_count * tile_width
        col_start = tile_index[slot_index, 1] // col_count * tile_width

        def apply(state, current_tile=current_tile, row_start=row_start, col_start=col_start):
            right = lax.dynamic_slice_in_dim(col_probes, col_start, tile_width, 1)
            forward = lax.dot_general(
                right, current_tile, (((1,), (1,)), ((), ())), preferred_element_type=jnp.float32
            )
            left = lax.dynamic_slice_in_dim(row_probes, row_start, tile_width, 1)
            mirror = jnp.dot(left, current_tile, preferred_element_type=jnp.float32)
            return (add_span(state[0], forward, row_start), add_span(state[1], mirror, col_start))

        partials = lax.cond(tile_index[slot_index, 2] > 0, apply, keep_same, partials)
    return partials


def shards(probe_block, prior_blocks, self_relatedness, tile_values, tile_index):
    col_count = lax.axis_size("col")
    blocks = prior_blocks.shape[0] + 1
    depth = probe_block.shape[0]
    basis = jnp.concatenate([prior_blocks, probe_block[None]], axis=0).reshape(blocks * depth, -1)
    gram = lax.psum(jnp.dot(basis, basis.T, preferred_element_type=jnp.float32), ("row", "col"))
    gram = gram.reshape(blocks, depth, blocks, depth)
    diagonal = jnp.stack([gram[b, :, b] for b in range(blocks)])
    eye = jnp.broadcast_to(jnp.eye(depth, dtype=jnp.float32), diagonal.shape)
    inverse = jax.scipy.linalg.cho_solve((jnp.linalg.cholesky(diagonal), True), eye)
    row_probes = lax.all_gather(probe_block, "col", axis=1, tiled=True)
    col_probes = lax.all_gather(probe_block, "row", axis=1, tiled=True)
    row_part, col_part = tile_products(tile_values, tile_index, row_probes, col_probes, col_count)
    row_total = lax.psum_scatter(row_part, "col", scatter_dimension=1, tiled=True)
    col_total = lax.psum_scatter(col_part, "row", scatter_dimension=1, tiled=True)
    product = self_relatedness[None, :] * probe_block.astype(jnp.float32) + row_total + col_total
    wide = basis.astype(jnp.float32)
    along = lax.psum(jnp.dot(wide, product.T, precision=HIGH), ("row", "col")).reshape(blocks, depth, depth)
    solved = []
    for b in range(blocks):
        target = along[b]
        for a in range(b):
            target = target - jnp.dot(gram[b, :, a], solved[a], precision=HIGH)
        solved.append(jnp.dot(inverse[b], target, precision=HIGH))
    stacked = jnp.stack(solved)
    current = product - jnp.dot(stacked.reshape(blocks * depth, depth).T, wide, precision=HIGH)
    return (current, stacked)


def solution(mesh):
    in_specs = (
        P(None, ("row", "col")),
        P(None, None, ("row", "col")),
        P(("row", "col")),
        P(("row", "col"), None, None),
        P(("row", "col"), None),
    )
    out_specs = (P(None, ("row", "col")), P())
    return jax.shard_map(shards, mesh=mesh, in_specs=in_specs, out_specs=out_specs, check_vma=False)
```

time: 437 us -> 372 us (0.85)
  blocking collectives: 213 us -> 11.8 us
  waiting for transfers between devices: 83.9 us -> 228 us
  other arithmetic: 60.4 us -> 54.2 us
    psum x5 -> x0, blocking collectives: 202 us -> none  [shards(): gram_block, along = lax.psum((gram_local, along_local), ('row', 'col'))]
    psum x0 -> x1, waiting for transfers between devices: none -> 133 us  [shards(): lax.psum(jnp.dot(wide, product.T, precision=HIGH), ('row', 'col'))]
    reduce_scatter x2, waiting for transfers between devices: 82.6 us -> 94.2 us  [the longest x1 55.9 us: shards(): lax.psum_scatter(col_part, 'row', scatter_dimension=1, tiled=True)]
    dot_general x15 -> x18, matrix products: 6.46 us -> 15.1 us  [the longest x10 9.95 us: shards(): target = target - jnp.dot(gram[b, :, a], solved[a], precision=HIGH)]
    dynamic_update_slice x6 -> x2, local copies, waits for them, and re-layouts: 10.6 us -> 3.63 us  [add_span(): return lax.dynamic_update_slice_in_dim(running, current + addend, offset, 1)]
    another operation x25 -> x7, other arithmetic: 60.3 us -> 54.1 us  [the longest x4 29.5 us: shards(): jnp.linalg.cholesky(diagonal)]
    dot_general x3 -> x1, matrix products: 7.05 us -> 2.34 us  [apply(): lax.dot_general(right, current_tile, (((1,), (1,)), ((), ())), preferred_...]
    dot_general x3 -> x1, matrix products: 6.59 us -> 2.2 us  [apply(): mirror = jnp.dot(left, current_tile, preferred_element_type=jnp.float32)]
  transfers between devices with their start and end apart: 3 -> 4, of which waited for: 2 -> 3; matrix products, arithmetic and copies ran while one was open for 2% -> 3% of each run, Pallas kernels for 0% -> 0%
where the time goes in v1:
time: 372 us; the launch traced here: 369 us
  waiting for transfers between devices  228 us (61%)
  other arithmetic  54.2 us (15%)
  between operations  34.8 us (9%)
  matrix products  20.3 us (5%)
  local copies, waits for them, and re-layouts  19.4 us (5%)
  blocking collectives  11.8 us (3%)
    psum x1, waiting for transfers between devices, shards(): lax.psum(jnp.dot(wide, product.T, precision=HIGH), ('row', 'col'))  133 us
    reduce_scatter x1, waiting for transfers between devices, shards(): lax.psum_scatter(col_part, 'row', scatter_dimension=1, tiled=True)  55.9 us
    reduce_scatter x1, waiting for transfers between devices, shards(): lax.psum_scatter(row_part, 'col', scatter_dimension=1, tiled=True)  38.3 us
    another operation x4, other arithmetic, shards(): jnp.linalg.cholesky(diagonal)  29.5 us
    another operation x3, other arithmetic, shards(): jax.scipy.linalg.cho_solve((jnp.linalg.cholesky(diagonal), True), eye)  24.7 us
    all_gather x1, blocking collectives, shards(): col_probes = lax.all_gather(probe_block, 'row', axis=1, tiled=True)  11.8 us
    dot_general x10, matrix products, shards(): target = target - jnp.dot(gram[b, :, a], solved[a], precision=HIGH)  9.95 us
  transfers between devices with their start and end apart: 4, of which 3 were waited for; matrix products, arithmetic and copies ran while one was open for 3% of the time, Pallas kernels for 0%

profile of v1, /device:TPU:0, one launch (start us, length us, event | category | flops | bytes accessed | tf_op | source)
XLA Modules:
  0.0 369.3 jit_solution(15840622651496221076)
XLA Ops:
  7.9 1.9 fusion.60
  30.6 11.8 %all_gather.6 = bf16[64,4096]{1,0:T(8,128)(2,1)S(1)} all-gather(bf16[64,1024]{1,0:T(8,128)(2,1)} %param.15), channel_id=1, replica_groups=mesh['row'=4,'col'=8] {'row'}, dimensions={1}, use_global_device_ids=true | all-gather | bytes 655360 | tf_op jit(solution)/shard_map/all_gather | solution.py:54
  42.5 5.7 %slice_bitcast_fusion = (bf16[1024,1024]{1,0:T(8,128)(2,1)S(1)}, bf16[1024,1024]{1,0:T(8,128)(2,1)}, bf16[1024,1024]{1,0:T(8,128)(2,1)}, bf16[1024,1024]{1,0:T(8,128)(2,1)}) fusion(bf16[5,1024,1024]{2,1,0:T(8,128)(2,1)} %param.18), kind=kLoop, calls=%fused_computation.38 | loop fusion | bytes 16777216 | tf_op jit(solution)/shard_map/squeeze | solution.py:26
  48.1 10.8 %conditional.5 = (f32[64,8192]{1,0:T(8,128)}, f32[64,4096]{1,0:T(8,128)}) conditional(s32[]{:T(128)} %bitcast.6, () %tuple.47, (s32[]{:T(128)}, bf16[64,4096]{1,0:T(8,128)(2,1)S(1)}, bf16[1024,1024]{1,0:T(8,128)(2,1)}, s32[]{:T(128)}, bf16[64,8192]{1,0:T(8,128)(2,1)}) %tuple.48), branch_computations={%region_0.0_spmd, %region_1.2_spmd} | conditional | flops 268435456 | bytes 9175148 | solution.py:39
  48.1 2.3 fusion.2
  50.5 1.5 broadcast_in_dim.19
  52.0 1.8 dynamic_update_slice.26
  53.8 2.2 fusion
  56.0 1.1 broadcast_in_dim.20
  57.1 1.8 dynamic_update_slice.27
  60.8 1.3 copy.12
  62.1 55.9 %reduce-scatter.5.cloned.1.call-done = f32[64,1024]{1,0:T(8,128)} async-done(((f32[64,4096]{1,0:T(8,128)}), f32[64,1024]{1,0:T(8,128)}) %reduce-scatter.5.cloned.1.call-update) | async-done | bytes 262160 | tf_op jit(solution)/shard_map/reduce_scatter | solution.py:57
  118.0 38.3 %reduce-scatter.3.cloned.1.call-done = f32[64,1024]{1,0:T(8,128)} async-done(((f32[64,8192]{1,0:T(8,128)}), f32[64,1024]{1,0:T(8,128)}) %reduce-scatter.3.cloned.1.call-update) | async-done | bytes 262160 | tf_op jit(solution)/shard_map/reduce_scatter | solution.py:56
  156.3 2.4 fusion.58
  158.8 132.7 %all-reduce.3.cloned.1.call-done = (f32[320,64]{0,1:T(8,128)}, f32[5,64,5,64]{1,3,2,0:T(8,128)}) async-done(((f32[320,64]{0,1:T(8,128)}, f32[5,64,5,64]{1,3,2,0:T(8,128)}), (f32[320,64]{0,1:T(8,128)}, f32[5,64,5,64]{1,3,2,0:T(8,128)})) %all-reduce.3.cloned.1.call-update) | async-done | bytes 491536 | tf_op jit(solution)/shard_map/psum | solution.py:60
  291.5 0.8 fusion.57
  292.3 0.8 fusion.56
  293.1 0.8 fusion.55
  294.6 0.8 fusion.53
  295.5 29.3 %custom-call.11 = f32[5,64,64]{2,1,0:T(8,128)S(1)} custom-call(f32[5,64,64]{2,1,0:T(8,128)S(1)} %fusion.46), custom_call_target="Cholesky" | custom-call | tf_op jit(solution)/shard_map/jit(cholesky)/cholesky | solution.py:52
  325.1 24.6 %custom-call.12 = f32[5,1,64,64]{2,3,1,0:T(8,128)S(1)} custom-call(f32[5,1,64,64]{3,2,1,0:T(8,128)S(1)} %select_bitcast_fusion), custom_call_target="InvertDiagBlocksLowerTriangular" | custom-call | tf_op jit(solution)/shard_map/jit(_cho_solve)/vmap()/triangular_solve | solution.py:52
  350.7 1.0 convolution_subtract_fusion.3
  351.7 1.0 convolution_subtract_fusion.9
  352.7 1.0 convolution_subtract_fusion.8
  353.7 1.0 convolution_subtract_fusion.6
  354.9 1.0 convolution_subtract_fusion.2
  355.9 1.0 convolution_subtract_fusion.7
  356.9 1.0 convolution_subtract_fusion.5
  358.1 1.0 convolution_subtract_fusion.1
  359.1 1.0 convolution_subtract_fusion.4
  360.3 1.0 convolution_subtract_fusion
  361.5 1.3 fusion.40
  (46 shorter events, 5.5 us)
Async XLA Ops:
  7.2 41.0 %all-gather.2.cloned.1.call-start = ((), (), s32[]{:S(2)}) async-start(), calls=%async_computation.2 | async-start | bytes 1179648 | tf_op jit(solution)/shard_map/all_gather | solution.py:53
  7.9 110.1 %reduce-scatter.5.cloned.1.call-start = ((), (), s32[]{:S(2)}) async-start(), calls=%async_computation.4 | async-start | bytes 1310720 | tf_op jit(solution)/shard_map/reduce_scatter | solution.py:57
  58.9 1.0 copy-start
  58.9 1.1 copy-start.1
  59.0 97.3 %reduce-scatter.3.cloned.1.call-start = ((), (), s32[]{:S(2)}) async-start(), calls=%async_computation.3 | async-start | bytes 2359296 | tf_op jit(solution)/shard_map/reduce_scatter | solution.py:56
  59.7 231.8 %all-reduce.3.cloned.1.call-start = ((), (), s32[]{:S(2)}) async-start(), calls=%async_computation.5 | async-start | bytes 1835008 | tf_op jit(solution)/shard_map/psum | solution.py:60
  60.6 95.7 %copy-start.6 = (f32[1024]{0:T(1024)S(1)}, f32[1024]{0:T(1024)}, u32[]{:S(2)}) copy-start(f32[1024]{0:T(1024)} %param.17) | copy-start | bytes 12292
  291.5 59.0 %copy-start.4 = (f32[320,64]{0,1:T(8,128)S(1)}, f32[320,64]{0,1:T(8,128)}, u32[]{:S(2)}) copy-start(f32[320,64]{0,1:T(8,128)} %get-tuple-element.328) | copy-start | bytes 245764
  294.6 66.9 %copy-start.2 = (f32[64,1024]{1,0:T(8,128)S(1)}, f32[64,1024]{1,0:T(8,128)}, u32[]{:S(2)}) copy-start(f32[64,1024]{1,0:T(8,128)} %reduce-scatter.5.cloned.1.call-done) | copy-start | bytes 786436
  294.6 66.9 %copy-start.3 = (f32[64,1024]{1,0:T(8,128)S(1)}, f32[64,1024]{1,0:T(8,128)}, u32[]{:S(2)}) copy-start(f32[64,1024]{1,0:T(8,128)} %reduce-scatter.3.cloned.1.call-done) | copy-start | bytes 786436
  361.5 1.3 copy-start.5
Sparse Core Ops, SparseCore 0:
  9.6 24.7 all-gather.1
  59.1 58.9 reduce-scatter.4
  120.4 35.8 reduce-scatter.2
  163.0 128.4 all-reduce.2

commit v2 on v1

v2 whole, which is shorter than its diff:
```python
import functools

import jax
import jax.numpy as jnp
from jax import lax
from jax.experimental import pallas as pl
from jax.experimental.pallas import tpu as pltpu
from jax.sharding import PartitionSpec as P

HIGH = lax.Precision.HIGHEST
MESH = pl.DeviceIdType.MESH
F32 = jnp.float32
BF16 = jnp.bfloat16
NT = (((1,), (1,)), ((), ()))
TN = (((0,), (0,)), ((), ()))


def round_up(value, unit):
    return -(-value // unit) * unit


def split3(x):
    hi = x.astype(BF16)
    rest = x - hi.astype(F32)
    mid = rest.astype(BF16)
    lo = (rest - mid.astype(F32)).astype(BF16)
    return hi, mid, lo


def lane_of(shape):
    return lax.broadcasted_iota(jnp.int32, shape, len(shape) - 1)


def pack(block):
    half = block.shape[0] // 2
    return jnp.where(lane_of((half, block.shape[1])) < block.shape[1] // 2, block[:half], block[half:])


def unpack(packed):
    width = packed.shape[1] // 2
    return jnp.concatenate([packed[:, :width], pltpu.roll(packed, width, 1)[:, :width]], axis=0)


def kernel(
    R, C, S, B, K, g_rows, h_rows,
    index_ref, probe_ref, prior_ref, self_ref, tiles_ref,
    out_ref, coef_ref,
    tile_buf, basis, rowp, colp, fwd, mir, row_part, sib_in, z_send, z_in, col_part, col_in,
    g_buf, g1, g2, g2_in, g3, g4, h_buf, h1, h2, h2_in, h3, h4, aug, mult,
    tile_sem, gz_s, gz_r, gs_s, gs_r, gr_s, gr_r, sb_s, sb_r, zz_s, zz_r, cc_s, cc_r, red_row_s, red_row_r, red_col_s, red_col_r,
):
    Z = C // 2
    r, c = lax.axis_index("row"), lax.axis_index("col")
    z, core = c // 2, c % 2
    sib = z * 2 + (1 - core)
    pairs = [(b, a) for a in range(B) for b in range(a, B)]

    def local(s):
        return pltpu.make_async_copy(tiles_ref.at[s], tile_buf.at[s], tile_sem.at[s])

    def remote(src, dst, ssem, rsem, row, col):
        return pltpu.make_async_remote_copy(
            src_ref=src, dst_ref=dst, send_sem=ssem, recv_sem=rsem, device_id=(row, col), device_id_type=MESH
        )

    def loop(n, body):
        def step(k, carry):
            body(k)
            return carry

        lax.fori_loop(0, n, step, 0)

    loop(S, lambda s: local(s).start())

    barrier = pltpu.get_barrier_semaphore()
    loop(C - 1, lambda k: pl.semaphore_signal(barrier, inc=1, device_id=(r, (c + 1 + k) % C), device_id_type=MESH))
    loop(R - 1, lambda k: pl.semaphore_signal(barrier, inc=1, device_id=((r + 1 + k) % R, c), device_id_type=MESH))
    pl.semaphore_wait(barrier, C + R - 2)

    def row_gather(k):
        peer = (r + 1 + k) % R
        return remote(probe_ref, colp.at[r], gr_s.at[peer], gr_r.at[r], peer, c)

    def z_gather(k):
        peer = (z + 1 + k) % Z
        return remote(probe_ref, rowp.at[c], gz_s.at[peer], gz_r.at[z], r, peer * 2 + core)

    def sib_gather(zz):
        slot = zz * 2 + core
        return remote(rowp.at[slot], rowp.at[slot], gs_s.at[zz], gs_r.at[zz], r, sib)

    def sib_arrival(zz):
        slot = zz * 2 + (1 - core)
        return remote(rowp.at[slot], rowp.at[slot], gs_s.at[zz], gs_r.at[zz], r, sib)

    loop(R - 1, lambda k: row_gather(k).start())
    loop(Z - 1, lambda k: z_gather(k).start())
    rowp[c] = probe_ref[...]
    colp[r] = probe_ref[...]
    sib_gather(z).start()

    def reducer(which, buf, in1, buf2, in2, all3, all4, rows):
        chunk = C * rows

        def p1(k):
            peer = (r + 1 + k) % R
            src = buf.at[pl.ds(pl.multiple_of(peer * chunk, 8), chunk)]
            return remote(src, in1.at[r], red_row_s.at[which, 0, peer], red_row_r.at[which, 0, r], peer, c)

        def p2(k):
            peer = (c + 1 + k) % C
            src = buf2.at[pl.ds(pl.multiple_of(peer * rows, 8), rows)]
            return remote(src, in2.at[c], red_col_s.at[which, 0, peer], red_col_r.at[which, 0, c], r, peer)

        def p3(k):
            peer = (c + 1 + k) % C
            return remote(all3.at[c], all3.at[c], red_col_s.at[which, 1, peer], red_col_r.at[which, 1, c], r, peer)

        def p4(k):
            peer = (r + 1 + k) % R
            return remote(all3, all4.at[r], red_row_s.at[which, 1, peer], red_row_r.at[which, 1, r], peer, c)

        def got_row(phase, dst, k):
            peer = (r + 1 + k) % R
            remote(dst.at[peer], dst.at[peer], red_row_s.at[which, phase, peer], red_row_r.at[which, phase, peer], peer, c).wait_recv()

        def got_col(phase, dst, k):
            peer = (c + 1 + k) % C
            remote(dst.at[peer], dst.at[peer], red_col_s.at[which, phase, peer], red_col_r.at[which, phase, peer], r, peer).wait_recv()

        def first():
            loop(R - 1, lambda k: p1(k).start())

        def second():
            buf2[...] = buf[pl.ds(pl.multiple_of(r * chunk, 8), chunk), :]

            def add(k):
                got_row(0, in1, k)
                buf2[...] += in1[(r + 1 + k) % R]

            loop(R - 1, add)
            loop(C - 1, lambda k: p2(k).start())

        def third():
            def add(k, total):
                got_col(0, in2, k)
                return total + in2[(c + 1 + k) % C]

            all3[c] = lax.fori_loop(0, C - 1, add, buf2[pl.ds(pl.multiple_of(c * rows, 8), rows), :])
            loop(C - 1, lambda k: p3(k).start())

        def fourth():
            loop(C - 1, lambda k: got_col(1, all3, k))
            loop(R - 1, lambda k: p4(k).start())
            all4[r] = all3[...]

        def fifth():
            loop(R - 1, lambda k: got_row(1, all4, k))

        def drain():
            loop(R - 1, lambda k: p1(k).wait_send())
            loop(C - 1, lambda k: p2(k).wait_send())
            loop(C - 1, lambda k: p3(k).wait_send())
            loop(R - 1, lambda k: p4(k).wait_send())

        return first, second, third, fourth, fifth, drain

    gram = reducer(0, g_buf, g1, g2, g2_in, g3, g4, g_rows)
    along = reducer(1, h_buf, h1, h2, h2_in, h3, h4, h_rows)

    for b in range(B - 1):
        basis[b * K : (b + 1) * K, :] = prior_ref[b]
    basis[(B - 1) * K :, :] = probe_ref[...]
    half = K // 2
    used = len(pairs) * half
    spot = 0
    for a in range(B):
        one = basis[a * K : (a + 1) * K, :]
        both = jnp.concatenate([one, one], axis=0)
        blocks = lax.dot_general(basis[a * K :, :], both, NT, preferred_element_type=F32)
        for b in range(a, B):
            g_buf[spot : spot + half, :] = pack(blocks[(b - a) * K : (b - a + 1) * K])
            spot += half
    if g_buf.shape[0] > used:
        g_buf[used:, :] = jnp.zeros((g_buf.shape[0] - used, 2 * K), F32)
    if h_buf.shape[0] > B * half:
        h_buf[B * half :, :] = jnp.zeros((h_buf.shape[0] - B * half, 2 * K), F32)
    gram[0]()

    def got_row_probe(k):
        peer = (r + 1 + k) % R
        remote(colp.at[peer], colp.at[peer], gr_s.at[peer], gr_r.at[peer], peer, c).wait_recv()

    loop(R - 1, got_row_probe)

    def forward(s):
        local(s).wait()
        right = colp[index_ref[s, 1] // C]
        fwd[s] = lax.dot_general(right, tile_buf[s], NT, preferred_element_type=F32)

    loop(S, forward)

    def share_probe(k):
        peer = (z + 1 + k) % Z
        slot = peer * 2 + core
        remote(rowp.at[slot], rowp.at[slot], gz_s.at[peer], gz_r.at[peer], r, slot).wait_recv()
        sib_gather(peer).start()

    loop(Z - 1, share_probe)
    gram[1]()

    def pick(parts, column, number, modulus, divide):
        def add(s, total):
            value = index_ref[s, column]
            place = value // C if divide else value % C
            hit = jnp.logical_and(place == number, index_ref[s, 2] > 0)
            return total + jnp.where(hit, parts[s], 0.0)

        return lax.fori_loop(0, S, add, jnp.zeros(parts.shape[1:], F32))

    def to_sib(zz):
        return remote(row_part.at[zz], sib_in.at[zz], sb_s.at[zz], sb_r.at[zz], r, sib)

    def give_sib(k):
        zz = (z + 1 + k) % Z
        row_part[zz] = pick(fwd, 0, zz * 2 + (1 - core), C, False)
        to_sib(zz).start()

    loop(Z, give_sib)

    def to_z(zz):
        return remote(z_send.at[zz], z_in.at[z], zz_s.at[zz], zz_r.at[z], r, zz * 2 + core)

    def chip_sum(zz):
        mine = pick(fwd, 0, zz * 2 + core, C, False)
        to_sib(zz).wait_recv()
        z_send[zz] = mine + sib_in[zz]

    def give_z(k):
        zz = (z + 1 + k) % Z
        chip_sum(zz)
        to_z(zz).start()

    loop(Z - 1, give_z)

    loop(Z, lambda zz: sib_arrival(zz).wait_recv())

    def mirror(s):
        left = rowp[index_ref[s, 0] % C]
        mir[s] = jnp.dot(left, tile_buf[s], preferred_element_type=F32)

    loop(S, mirror)

    def to_row(peer):
        return remote(col_part.at[peer], col_in.at[r], cc_s.at[peer], cc_r.at[r], peer, c)

    def give_row(k):
        peer = (r + 1 + k) % R
        col_part[peer] = pick(mir, 1, peer, C, True)
        to_row(peer).start()

    loop(R - 1, give_row)
    gram[2]()
    chip_sum(z)
    out_ref[...] = (
        self_ref[...] * probe_ref[...].astype(F32) + z_send[z] + pick(mir, 1, r, C, True)
    )
    gram[3]()
    gram[4]()

    sums = g4[...].reshape(-1, 2 * K)
    gram_blocks = {}
    lanes = lane_of((K, 2 * K))
    down = lax.broadcasted_iota(jnp.int32, (K, 2 * K), 0)
    eye = jnp.where(lanes == down + K, 1.0, 0.0)
    for i, (b, a) in enumerate(pairs):
        packed = sums[i * half : (i + 1) * half]
        if a == b:
            whole = jnp.concatenate([packed, pltpu.roll(packed, K, 1)], axis=0)
            aug[b] = jnp.where(lanes < K, whole, eye)
        else:
            gram_blocks[b, a] = unpack(packed)

    all_lanes = lane_of((B, K, 2 * K))
    all_down = lax.broadcasted_iota(jnp.int32, (B, K, 2 * K), 1)
    row_lanes = lane_of((B, 1, 2 * K))

    def eliminate(k):
        whole = aug[...]
        row = aug[:, pl.ds(k, 1), :]
        column = jnp.sum(jnp.where(all_lanes == k, whole, 0.0), axis=2, keepdims=True)
        pivot = jnp.sum(jnp.where(row_lanes == k, row, 0.0), axis=2, keepdims=True)
        scaled = row / pivot
        aug[...] = jnp.where(all_down == k, scaled, whole - column * scaled)

    loop(K, eliminate)
    inverse = [pltpu.roll(aug[b], K, 1)[:, :K] for b in range(B)]
    for i, (b, a) in enumerate(pairs):
        if a != b:
            mult[i] = jnp.dot(inverse[b], gram_blocks[b, a], precision=HIGH, preferred_element_type=F32)

    def add_row(k):
        peer = (r + 1 + k) % R
        remote(col_in.at[peer], col_in.at[peer], cc_s.at[peer], cc_r.at[peer], peer, c).wait_recv()
        out_ref[...] += col_in[peer]

    loop(R - 1, add_row)

    def add_z(k):
        peer = (z + 1 + k) % Z
        remote(z_in.at[peer], z_in.at[peer], zz_s.at[peer], zz_r.at[peer], r, peer * 2 + core).wait_recv()
        out_ref[...] += z_in[peer]

    loop(Z - 1, add_z)

    product = out_ref[...]
    inner = jnp.zeros((B * K, 2 * K), F32)
    for part in split3(product)[::-1]:
        both = jnp.concatenate([part, part], axis=0)
        inner = inner + lax.dot_general(basis[...], both, NT, preferred_element_type=F32)
    for b in range(B):
        h_buf[b * half : (b + 1) * half, :] = pack(inner[b * K : (b + 1) * K])
    for phase in along[:5]:
        phase()
    targets = h4[...].reshape(-1, 2 * K)
    solved = []
    for b in range(B):
        target = unpack(targets[b * half : (b + 1) * half])
        value = jnp.dot(inverse[b], target, precision=HIGH, preferred_element_type=F32)
        for a in range(b):
            value = value - jnp.dot(mult[pairs.index((b, a))], solved[a], precision=HIGH, preferred_element_type=F32)
        solved.append(value)
        coef_ref[b] = value
    stacked = jnp.concatenate(solved, axis=0)
    taken = jnp.zeros(product.shape, F32)
    for part in split3(stacked.T)[::-1]:
        taken = taken + jnp.dot(part, basis[...], preferred_element_type=F32)
    out_ref[...] = product - taken

    gram[5]()
    along[5]()
    loop(R - 1, lambda k: row_gather(k).wait_send())
    loop(Z - 1, lambda k: z_gather(k).wait_send())
    loop(Z, lambda zz: sib_gather(zz).wait_send())
    loop(Z, lambda zz: to_sib(zz).wait_send())
    loop(Z - 1, lambda k: to_z((z + 1 + k) % Z).wait_send())
    loop(R - 1, lambda k: to_row((r + 1 + k) % R).wait_send())


def shards(R, C, probe_block, prior_blocks, self_relatedness, tile_values, tile_index):
    K, T = probe_block.shape
    S = tile_values.shape[0]
    B = prior_blocks.shape[0] + 1
    Z = C // 2
    half = K // 2
    g_rows = round_up(-(-(B * (B + 1) // 2 * half) // (R * C)), 8)
    h_rows = round_up(-(-(B * half) // (R * C)), 8)
    vmem = lambda shape, dtype=F32: pltpu.VMEM(shape, dtype)
    dma = lambda *shape: pltpu.SemaphoreType.DMA(shape)
    W = 2 * K

    def reduce_scratch(rows):
        return [
            vmem((R * C * rows, W)), vmem((R, C * rows, W)), vmem((C * rows, W)),
            vmem((C, rows, W)), vmem((C, rows, W)), vmem((R, C, rows, W)),
        ]

    scratch = [
        vmem((S, T, T), BF16), vmem((B * K, T), BF16), vmem((C, K, T), BF16), vmem((R, K, T), BF16),
        vmem((S, K, T)), vmem((S, K, T)),
        vmem((Z, K, T)), vmem((Z, K, T)), vmem((Z, K, T)), vmem((Z, K, T)),
        vmem((R, K, T)), vmem((R, K, T)),
        *reduce_scratch(g_rows), *reduce_scratch(h_rows),
        vmem((B, K, W)), vmem((B * (B + 1) // 2, K, K)),
        dma(S), dma(Z), dma(Z), dma(Z), dma(Z), dma(R), dma(R), dma(Z), dma(Z), dma(Z), dma(Z), dma(R), dma(R),
        dma(2, 2, R), dma(2, 2, R), dma(2, 2, C), dma(2, 2, C),
    ]
    in_vmem = pl.BlockSpec(memory_space=pltpu.VMEM)
    residual, coefficients = pl.pallas_call(
        functools.partial(kernel, R, C, S, B, K, g_rows, h_rows),
        out_shape=(jax.ShapeDtypeStruct((K, T), F32), jax.ShapeDtypeStruct((B, K, K), F32)),
        in_specs=[
            pl.BlockSpec(memory_space=pltpu.SMEM), in_vmem, in_vmem, in_vmem, pl.BlockSpec(memory_space=pl.ANY),
        ],
        out_specs=(in_vmem, in_vmem),
        scratch_shapes=scratch,
        compiler_params=pltpu.CompilerParams(
            collective_id=0, has_side_effects=True, vmem_limit_bytes=56 * 1024 * 1024
        ),
        cost_estimate=pl.CostEstimate(
            flops=4 * S * K * T * T, bytes_accessed=2 * S * T * T, transcendentals=0
        ),
    )(tile_index, probe_block, prior_blocks, self_relatedness[None], tile_values)
    return (residual, coefficients)


def solution(mesh):
    in_specs = (
        P(None, ("row", "col")),
        P(None, None, ("row", "col")),
        P(("row", "col")),
        P(("row", "col"), None, None),
        P(("row", "col"), None),
    )
    out_specs = (P(None, ("row", "col")), P())
    body = functools.partial(shards, mesh.shape["row"], mesh.shape["col"])
    return jax.shard_map(body, mesh=mesh, in_specs=in_specs, out_specs=out_specs, check_vma=False)
```

time: 372 us -> 86.5 us (0.23)
  waiting for transfers between devices: 228 us -> 0 us
  Pallas kernels: 0 us -> 81.1 us
  other arithmetic: 54.2 us -> 0 us
  between operations: 34.8 us -> 0.64 us
  matrix products: 20.3 us -> 0 us
  local copies, waits for them, and re-layouts: 19.4 us -> 4.62 us
  blocking collectives: 11.8 us -> 0 us
    psum x1 -> x0, waiting for transfers between devices: 133 us -> none  [shards(): lax.psum(jnp.dot(wide, product.T, precision=HIGH), ('row', 'col'))]
    reduce_scatter x2 -> x0, waiting for transfers between devices: 94.2 us -> none  [the longest x1 55.9 us: shards(): lax.psum_scatter(col_part, 'row', scatter_dimension=1, tiled=True)]
    pallas_call x0 -> x1, Pallas kernels: none -> 81.1 us  [shards(): pl.pallas_call(functools.partial(kernel, R, C, S, B, K, g_rows, h_rows),...]
    another operation x7 -> x0, other arithmetic: 54.1 us -> none  [the longest x4 29.5 us: shards(): jnp.linalg.cholesky(diagonal)]
    dot_general x20 -> x0, matrix products: 19.6 us -> none  [the longest x10 9.95 us: shards(): target = target - jnp.dot(gram[b, :, a], solved[a], precision=HIGH)]
    all_gather x1 -> x0, blocking collectives: 11.8 us -> none  [shards(): col_probes = lax.all_gather(probe_block, 'row', axis=1, tiled=True)]
    squeeze x1 -> x0, local copies, waits for them, and re-layouts: 5.67 us -> none  [tile_products(): current_tile = tile_values[slot_index]]
  transfers between devices with their start and end apart: 4 -> 0, of which waited for: 3 -> 0; matrix products, arithmetic and copies ran while one was open for 3% -> 0% of each run, Pallas kernels for 0% -> 0%
where the time goes in v2:
time: 86.5 us; the launch traced here: 86.3 us
  Pallas kernels  81.1 us (94%)
  local copies, waits for them, and re-layouts  4.62 us (5%)
    pallas_call x1, Pallas kernels, shards(): pl.pallas_call(functools.partial(kernel, R, C, S, B, K, g_rows, h_rows),...  81.1 us
    unnamed x3, local copies, waits for them, and re-layouts  4.62 us

profile of v2, /device:TPU:0, one launch (start us, length us, event | category | flops | bytes accessed | tf_op | source)
XLA Modules:
  0.0 86.3 jit_solution(428544221154877476)
XLA Ops:
  0.6 1.4 %copy.7.index_ref = s32[5,3]{1,0:T(8,128)} copy(s32[5,3]{0,1:T(4,128)} %param.9) | data formatting | bytes 120 | tf_op args[4]
  2.0 81.1 %shard_map.68 = (f32[64,1024]{1,0:T(8,128)}, f32[5,64,64]{2,1,0:T(8,128)}) custom-call(s32[5,3]{1,0:T(8,128)} %copy.7.index_ref, bf16[64,1024]{1,0:T(8,128)(2,1)} %probe_ref.1, bf16[4,64,1024]{2,1,0:T(8,128)(2,1)} %prior_ref.1, f32[1,1024]{1,0:T(1,128)} %bitcast.1, bf16[5,1024,1024]{2,1,0:T(8,128)(2,1)} %tiles_ref.1), custom_call_target="tpu_custom_call" | custom-call | flops 1342177280 | bytes 10485760 | tf_op jit(solution)/shard_map/pallas_call | solution.py:379
  83.1 1.7 %copy.10 = f32[64,1024]{1,0:T(8,128)} copy(f32[64,1024]{1,0:T(8,128)} %get-tuple-element.4) | data formatting | bytes 524288
  84.7 1.6 %copy.11 = f32[5,64,64]{2,1,0:T(8,128)} copy(f32[5,64,64]{2,1,0:T(8,128)} %get-tuple-element.5) | data formatting | bytes 163840

commit v3 on v2

--- a/solution.py
+++ b/solution.py
@@ -11,8 +11,8 @@
 MESH = pl.DeviceIdType.MESH
 F32 = jnp.float32
 BF16 = jnp.bfloat16
+I16 = jnp.int16
 NT = (((1,), (1,)), ((), ()))
-TN = (((0,), (0,)), ((), ()))
 
 
 def round_up(value, unit):
@@ -41,13 +41,32 @@
     return jnp.concatenate([packed[:, :width], pltpu.roll(packed, width, 1)[:, :width]], axis=0)
 
 
+def code(block):
+    rows = block.shape[0]
+    most = jnp.maximum(jnp.max(jnp.abs(block), axis=1, keepdims=True), 1e-30)
+    quantized = jnp.round(block * (32767.0 / most)).astype(jnp.int32).astype(jnp.int16)
+    shape = (rows, 128)
+    hit = lane_of(shape) == lax.broadcasted_iota(jnp.int32, shape, 0)
+    line = jnp.sum(jnp.where(hit, most * (1.0 / 32767.0), 0.0), axis=0, keepdims=True)
+    return quantized, jnp.broadcast_to(line, (8, 128))
+
+
+def decode(quantized, lines):
+    shape = (quantized.shape[0], 128)
+    hit = lane_of(shape) == lax.broadcasted_iota(jnp.int32, shape, 0)
+    scale = jnp.sum(jnp.where(hit, lines[:1], 0.0), axis=1, keepdims=True)
+    return quantized.astype(jnp.int32).astype(F32) * scale
+
+
 def kernel(
     R, C, S, B, K, g_rows, h_rows,
-    index_ref, probe_ref, prior_ref, self_ref, tiles_ref,
+    index_in, probe_ref, prior_ref, self_ref, tiles_ref,
     out_ref, coef_ref,
-    tile_buf, basis, rowp, colp, fwd, mir, row_part, sib_in, z_send, z_in, col_part, col_in,
-    g_buf, g1, g2, g2_in, g3, g4, h_buf, h1, h2, h2_in, h3, h4, aug, mult,
-    tile_sem, gz_s, gz_r, gs_s, gs_r, gr_s, gr_r, sb_s, sb_r, zz_s, zz_r, cc_s, cc_r, red_row_s, red_row_r, red_col_s, red_col_r,
+    index_ref, tile_buf, basis, rowp, colp, fwd, mir, row_part, sib_in, z_sum, z_send, z_in, z_send_scale, z_in_scale,
+    col_send, col_in, col_send_scale, col_in_scale,
+    g_buf, g1, g2, g2_in, g3, g4, h_buf, h1, h2, h3, aug, solver,
+    index_sem, tile_sem, gz_s, gz_r, gs_s, gs_r, gr_s, gr_r, sb_s, sb_r, zz_s, zz_r, zs_s, zs_r, cc_s, cc_r, cs_s, cs_r,
+    red_row_s, red_row_r, red_col_s, red_col_r, al_row_s, al_row_r, al_col_s, al_col_r,
 ):
     Z = C // 2
     r, c = lax.axis_index("row"), lax.axis_index("col")
@@ -70,6 +89,8 @@
 
         lax.fori_loop(0, n, step, 0)
 
+    index_copy = pltpu.make_async_copy(index_in, index_ref, index_sem)
+    index_copy.start()
     loop(S, lambda s: local(s).start())
 
     barrier = pltpu.get_barrier_semaphore()
@@ -99,34 +120,34 @@
     colp[r] = probe_ref[...]
     sib_gather(z).start()
 
-    def reducer(which, buf, in1, buf2, in2, all3, all4, rows):
+    def reducer(buf, in1, buf2, in2, all3, all4, rows):
         chunk = C * rows
 
         def p1(k):
             peer = (r + 1 + k) % R
             src = buf.at[pl.ds(pl.multiple_of(peer * chunk, 8), chunk)]
-            return remote(src, in1.at[r], red_row_s.at[which, 0, peer], red_row_r.at[which, 0, r], peer, c)
+            return remote(src, in1.at[r], red_row_s.at[0, peer], red_row_r.at[0, r], peer, c)
 
         def p2(k):
             peer = (c + 1 + k) % C
             src = buf2.at[pl.ds(pl.multiple_of(peer * rows, 8), rows)]
-            return remote(src, in2.at[c], red_col_s.at[which, 0, peer], red_col_r.at[which, 0, c], r, peer)
+            return remote(src, in2.at[c], red_col_s.at[0, peer], red_col_r.at[0, c], r, peer)
 
         def p3(k):
             peer = (c + 1 + k) % C
-            return remote(all3.at[c], all3.at[c], red_col_s.at[which, 1, peer], red_col_r.at[which, 1, c], r, peer)
+            return remote(all3.at[c], all3.at[c], red_col_s.at[1, peer], red_col_r.at[1, c], r, peer)
 
         def p4(k):
             peer = (r + 1 + k) % R
-            return remote(all3, all4.at[r], red_row_s.at[which, 1, peer], red_row_r.at[which, 1, r], peer, c)
+            return remote(all3, all4.at[r], red_row_s.at[1, peer], red_row_r.at[1, r], peer, c)
 
         def got_row(phase, dst, k):
             peer = (r + 1 + k) % R
-            remote(dst.at[peer], dst.at[peer], red_row_s.at[which, phase, peer], red_row_r.at[which, phase, peer], peer, c).wait_recv()
+            remote(dst.at[peer], dst.at[peer], red_row_s.at[phase, peer], red_row_r.at[phase, peer], peer, c).wait_recv()
 
         def got_col(phase, dst, k):
             peer = (c + 1 + k) % C
-            remote(dst.at[peer], dst.at[peer], red_col_s.at[which, phase, peer], red_col_r.at[which, phase, peer], r, peer).wait_recv()
+            remote(dst.at[peer], dst.at[peer], red_col_s.at[phase, peer], red_col_r.at[phase, peer], r, peer).wait_recv()
 
         def first():
             loop(R - 1, lambda k: p1(k).start())
@@ -165,8 +186,42 @@
 
         return first, second, third, fourth, fifth, drain
 
-    gram = reducer(0, g_buf, g1, g2, g2_in, g3, g4, g_rows)
-    along = reducer(1, h_buf, h1, h2, h2_in, h3, h4, h_rows)
+    gram = reducer(g_buf, g1, g2, g2_in, g3, g4, g_rows)
+
+    def a1(k):
+        peer = (c + 1 + k) % C
+        src = h_buf.at[pl.ds(pl.multiple_of(peer * h_rows, 8), h_rows)]
+        return remote(src, h1.at[c], al_col_s.at[0, peer], al_col_r.at[0, c], r, peer)
+
+    def a2(k):
+        peer = (r + 1 + k) % R
+        return remote(h2.at[r], h2.at[r], al_row_s.at[peer], al_row_r.at[r], peer, c)
+
+    def a3(k):
+        peer = (c + 1 + k) % C
+        return remote(h3.at[c], h3.at[c], al_col_s.at[1, peer], al_col_r.at[1, c], r, peer)
+
+    def got_a_col(phase, dst, k):
+        peer = (c + 1 + k) % C
+        remote(dst.at[peer], dst.at[peer], al_col_s.at[phase, peer], al_col_r.at[phase, peer], r, peer).wait_recv()
+
+    def got_a_row(k):
+        peer = (r + 1 + k) % R
+        remote(h2.at[peer], h2.at[peer], al_row_s.at[peer], al_row_r.at[peer], peer, c).wait_recv()
+
+    def reduce_along():
+        loop(C - 1, lambda k: a1(k).start())
+
+        def add(k, total):
+            got_a_col(0, h1, k)
+            return total + h1[(c + 1 + k) % C]
+
+        h2[r] = lax.fori_loop(0, C - 1, add, h_buf[pl.ds(pl.multiple_of(c * h_rows, 8), h_rows), :])
+        loop(R - 1, lambda k: a2(k).start())
+        loop(R - 1, got_a_row)
+        h3[c] = lax.fori_loop(1, R, lambda k, total: total + h2[k], h2[0])
+        loop(C - 1, lambda k: a3(k).start())
+        loop(C - 1, lambda k: got_a_col(1, h3, k))
 
     for b in range(B - 1):
         basis[b * K : (b + 1) * K, :] = prior_ref[b]
@@ -192,11 +247,12 @@
         remote(colp.at[peer], colp.at[peer], gr_s.at[peer], gr_r.at[peer], peer, c).wait_recv()
 
     loop(R - 1, got_row_probe)
+    index_copy.wait()
 
     def forward(s):
         local(s).wait()
         right = colp[index_ref[s, 1] // C]
-        fwd[s] = lax.dot_general(right, tile_buf[s], NT, preferred_element_type=F32)
+        fwd[s] = lax.dot_general(tile_buf[s], right, NT, preferred_element_type=F32).T
 
     loop(S, forward)
 
@@ -209,21 +265,28 @@
     loop(Z - 1, share_probe)
     gram[1]()
 
-    def pick(parts, column, number, modulus, divide):
-        def add(s, total):
-            value = index_ref[s, column]
+    def pick(dst, parts, column, number, divide):
+        hits = []
+        for slot in range(S):
+            value = index_ref[slot, column]
             place = value // C if divide else value % C
-            hit = jnp.logical_and(place == number, index_ref[s, 2] > 0)
-            return total + jnp.where(hit, parts[s], 0.0)
-
-        return lax.fori_loop(0, S, add, jnp.zeros(parts.shape[1:], F32))
+            hits.append(jnp.logical_and(place == number, index_ref[slot, 2] > 0))
+
+        def some(k):
+            rows = pl.ds(pl.multiple_of(k * 16, 16), 16)
+            total = jnp.where(hits[0], parts[0, rows, :], 0.0)
+            for slot in range(1, S):
+                total = total + jnp.where(hits[slot], parts[slot, rows, :], 0.0)
+            dst[rows, :] = total
+
+        loop(K // 16, some)
 
     def to_sib(zz):
         return remote(row_part.at[zz], sib_in.at[zz], sb_s.at[zz], sb_r.at[zz], r, sib)
 
     def give_sib(k):
         zz = (z + 1 + k) % Z
-        row_part[zz] = pick(fwd, 0, zz * 2 + (1 - core), C, False)
+        pick(row_part.at[zz], fwd, 0, zz * 2 + (1 - core), False)
         to_sib(zz).start()
 
     loop(Z, give_sib)
@@ -231,17 +294,22 @@
     def to_z(zz):
         return remote(z_send.at[zz], z_in.at[z], zz_s.at[zz], zz_r.at[z], r, zz * 2 + core)
 
+    def to_z_scale(zz):
+        return remote(z_send_scale.at[zz], z_in_scale.at[z], zs_s.at[zz], zs_r.at[z], r, zz * 2 + core)
+
     def chip_sum(zz):
-        mine = pick(fwd, 0, zz * 2 + core, C, False)
+        pick(z_sum, fwd, 0, zz * 2 + core, False)
         to_sib(zz).wait_recv()
-        z_send[zz] = mine + sib_in[zz]
+        return z_sum[...] + sib_in[zz]
 
     def give_z(k):
         zz = (z + 1 + k) % Z
-        chip_sum(zz)
+        z_send[zz], z_send_scale[zz] = code(chip_sum(zz))
         to_z(zz).start()
+        to_z_scale(zz).start()
 
     loop(Z - 1, give_z)
+    gram[2]()
 
     loop(Z, lambda zz: sib_arrival(zz).wait_recv())
 
@@ -251,21 +319,25 @@
 
     loop(S, mirror)
 
+    gram[3]()
+
     def to_row(peer):
-        return remote(col_part.at[peer], col_in.at[r], cc_s.at[peer], cc_r.at[r], peer, c)
+        return remote(col_send.at[peer], col_in.at[r], cc_s.at[peer], cc_r.at[r], peer, c)
+
+    def to_row_scale(peer):
+        return remote(col_send_scale.at[peer], col_in_scale.at[r], cs_s.at[peer], cs_r.at[r], peer, c)
 
     def give_row(k):
         peer = (r + 1 + k) % R
-        col_part[peer] = pick(mir, 1, peer, C, True)
+        pick(z_sum, mir, 1, peer, True)
+        col_send[peer], col_send_scale[peer] = code(z_sum[...])
         to_row(peer).start()
+        to_row_scale(peer).start()
 
     loop(R - 1, give_row)
-    gram[2]()
-    chip_sum(z)
-    out_ref[...] = (
-        self_ref[...] * probe_ref[...].astype(F32) + z_send[z] + pick(mir, 1, r, C, True)
-    )
-    gram[3]()
+    out_ref[...] = self_ref[...] * probe_ref[...].astype(F32) + chip_sum(z)
+    pick(z_sum, mir, 1, r, True)
+    out_ref[...] += z_sum[...]
     gram[4]()
 
     sums = g4[...].reshape(-1, 2 * K)
@@ -294,22 +366,35 @@
         aug[...] = jnp.where(all_down == k, scaled, whole - column * scaled)
 
     loop(K, eliminate)
-    inverse = [pltpu.roll(aug[b], K, 1)[:, :K] for b in range(B)]
-    for i, (b, a) in enumerate(pairs):
-        if a != b:
-            mult[i] = jnp.dot(inverse[b], gram_blocks[b, a], precision=HIGH, preferred_element_type=F32)
+    square = jnp.where(lane_of((K, K)) == lax.broadcasted_iota(jnp.int32, (K, K), 0), 1.0, 0.0)
+    for b in range(B):
+        line = [square]
+        if b > 0:
+            row = jnp.concatenate([gram_blocks[b, a] for a in range(b)], axis=1)
+            done = solver[: b * K, : b * K]
+            line = [-jnp.dot(row, done, precision=HIGH, preferred_element_type=F32), square]
+        if b < B - 1:
+            line.append(jnp.zeros((K, (B - 1 - b) * K), F32))
+        inverse = pltpu.roll(aug[b], K, 1)[:, :K]
+        solver[b * K : (b + 1) * K, :] = jnp.dot(
+            inverse, jnp.concatenate(line, axis=1), precision=HIGH, preferred_element_type=F32
+        )
 
     def add_row(k):
         peer = (r + 1 + k) % R
         remote(col_in.at[peer], col_in.at[peer], cc_s.at[peer], cc_r.at[peer], peer, c).wait_recv()
-        out_ref[...] += col_in[peer]
+        lines = col_in_scale.at[peer]
+        remote(lines, lines, cs_s.at[peer], cs_r.at[peer], peer, c).wait_recv()
+        out_ref[...] += decode(col_in[peer], col_in_scale[peer])
 
     loop(R - 1, add_row)
 
     def add_z(k):
         peer = (z + 1 + k) % Z
         remote(z_in.at[peer], z_in.at[peer], zz_s.at[peer], zz_r.at[peer], r, peer * 2 + core).wait_recv()
-        out_ref[...] += z_in[peer]
+        lines = z_in_scale.at[peer]
+        remote(lines, lines, zs_s.at[peer], zs_r.at[peer], r, peer * 2 + core).wait_recv()
+        out_ref[...] += decode(z_in[peer], z_in_scale[peer])
 
     loop(Z - 1, add_z)
 
@@ -320,31 +405,37 @@
         inner = inner + lax.dot_general(basis[...], both, NT, preferred_element_type=F32)
     for b in range(B):
         h_buf[b * half : (b + 1) * half, :] = pack(inner[b * K : (b + 1) * K])
-    for phase in along[:5]:
-        phase()
-    targets = h4[...].reshape(-1, 2 * K)
-    solved = []
-    for b in range(B):
-        target = unpack(targets[b * half : (b + 1) * half])
-        value = jnp.dot(inverse[b], target, precision=HIGH, preferred_element_type=F32)
-        for a in range(b):
-            value = value - jnp.dot(mult[pairs.index((b, a))], solved[a], precision=HIGH, preferred_element_type=F32)
-        solved.append(value)
-        coef_ref[b] = value
-    stacked = jnp.concatenate(solved, axis=0)
-    taken = jnp.zeros(product.shape, F32)
-    for part in split3(stacked.T)[::-1]:
-        taken = taken + jnp.dot(part, basis[...], preferred_element_type=F32)
-    out_ref[...] = product - taken
+    reduce_along()
+    targets = h3[...].reshape(-1, 2 * K)
+    stacked = jnp.concatenate([unpack(targets[b * half : (b + 1) * half]) for b in range(B)], axis=0)
+    solved = jnp.dot(solver[...], stacked, precision=HIGH, preferred_element_type=F32)
+    coef_ref[...] = solved.reshape(B, K, K)
 
     gram[5]()
-    along[5]()
+    loop(C - 1, lambda k: a1(k).wait_send())
+    loop(R - 1, lambda k: a2(k).wait_send())
+    loop(C - 1, lambda k: a3(k).wait_send())
     loop(R - 1, lambda k: row_gather(k).wait_send())
     loop(Z - 1, lambda k: z_gather(k).wait_send())
     loop(Z, lambda zz: sib_gather(zz).wait_send())
     loop(Z, lambda zz: to_sib(zz).wait_send())
     loop(Z - 1, lambda k: to_z((z + 1 + k) % Z).wait_send())
+    loop(Z - 1, lambda k: to_z_scale((z + 1 + k) % Z).wait_send())
     loop(R - 1, lambda k: to_row((r + 1 + k) % R).wait_send())
+    loop(R - 1, lambda k: to_row_scale((r + 1 + k) % R).wait_send())
+
+
+def finish(product_ref, coef_ref, prior_ref, probe_ref, out_ref, coef_out):
+    B, K, _ = coef_ref.shape
+    coef_out[...] = coef_ref[...]
+    stacked = coef_ref[...].reshape(B * K, K)
+    last = (B - 1) * K
+    taken = jnp.zeros(out_ref.shape, F32)
+    for part in split3(stacked.T)[::-1]:
+        for b in range(B - 1):
+            taken = taken + jnp.dot(part[:, b * K : (b + 1) * K], prior_ref[b], preferred_element_type=F32)
+        taken = taken + jnp.dot(part[:, last:], probe_ref[...], preferred_element_type=F32)
+    out_ref[...] = product_ref[...] - taken
 
 
 def shards(R, C, probe_block, prior_blocks, self_relatedness, tile_values, tile_index):
@@ -354,7 +445,7 @@
     Z = C // 2
     half = K // 2
     g_rows = round_up(-(-(B * (B + 1) // 2 * half) // (R * C)), 8)
-    h_rows = round_up(-(-(B * half) // (R * C)), 8)
+    h_rows = round_up(-(-(B * half) // C), 8)
     vmem = lambda shape, dtype=F32: pltpu.VMEM(shape, dtype)
     dma = lambda *shape: pltpu.SemaphoreType.DMA(shape)
     W = 2 * K
@@ -366,21 +457,24 @@
         ]
 
     scratch = [
-        vmem((S, T, T), BF16), vmem((B * K, T), BF16), vmem((C, K, T), BF16), vmem((R, K, T), BF16),
+        pltpu.SMEM(tile_index.shape, jnp.int32), vmem((S, T, T), BF16), vmem((B * K, T), BF16), vmem((C, K, T), BF16), vmem((R, K, T), BF16),
         vmem((S, K, T)), vmem((S, K, T)),
-        vmem((Z, K, T)), vmem((Z, K, T)), vmem((Z, K, T)), vmem((Z, K, T)),
-        vmem((R, K, T)), vmem((R, K, T)),
-        *reduce_scratch(g_rows), *reduce_scratch(h_rows),
-        vmem((B, K, W)), vmem((B * (B + 1) // 2, K, K)),
-        dma(S), dma(Z), dma(Z), dma(Z), dma(Z), dma(R), dma(R), dma(Z), dma(Z), dma(Z), dma(Z), dma(R), dma(R),
-        dma(2, 2, R), dma(2, 2, R), dma(2, 2, C), dma(2, 2, C),
+        vmem((Z, K, T)), vmem((Z, K, T)), vmem((K, T)),
+        vmem((Z, K, T), I16), vmem((Z, K, T), I16), vmem((Z, 8, 128)), vmem((Z, 8, 128)),
+        vmem((R, K, T), I16), vmem((R, K, T), I16), vmem((R, 8, 128)), vmem((R, 8, 128)),
+        *reduce_scratch(g_rows),
+        vmem((C * h_rows, W)), vmem((C, h_rows, W)), vmem((R, h_rows, W)), vmem((C, h_rows, W)),
+        vmem((B, K, W)), vmem((B * K, B * K)),
+        pltpu.SemaphoreType.DMA, dma(S), dma(Z), dma(Z), dma(Z), dma(Z), dma(R), dma(R), dma(Z), dma(Z),
+        dma(Z), dma(Z), dma(Z), dma(Z), dma(R), dma(R), dma(R), dma(R),
+        dma(2, R), dma(2, R), dma(2, C), dma(2, C), dma(R), dma(R), dma(2, C), dma(2, C),
     ]
     in_vmem = pl.BlockSpec(memory_space=pltpu.VMEM)
-    residual, coefficients = pl.pallas_call(
+    product, coefficients = pl.pallas_call(
         functools.partial(kernel, R, C, S, B, K, g_rows, h_rows),
         out_shape=(jax.ShapeDtypeStruct((K, T), F32), jax.ShapeDtypeStruct((B, K, K), F32)),
         in_specs=[
-            pl.BlockSpec(memory_space=pltpu.SMEM), in_vmem, in_vmem, in_vmem, pl.BlockSpec(memory_space=pl.ANY),
+            pl.BlockSpec(memory_space=pl.ANY), in_vmem, in_vmem, in_vmem, pl.BlockSpec(memory_space=pl.ANY),
         ],
         out_specs=(in_vmem, in_vmem),
         scratch_shapes=scratch,
@@ -391,7 +485,12 @@
             flops=4 * S * K * T * T, bytes_accessed=2 * S * T * T, transcendentals=0
         ),
     )(tile_index, probe_block, prior_blocks, self_relatedness[None], tile_values)
-    return (residual, coefficients)
+    return pl.pallas_call(
+        finish,
+        out_shape=(jax.ShapeDtypeStruct((K, T), F32), jax.ShapeDtypeStruct((B, K, K), F32)),
+        in_specs=[in_vmem] * 4,
+        out_specs=(in_vmem, in_vmem),
+    )(product, coefficients, prior_blocks, probe_block)
 
 
 def solution(mesh):

time: 86.5 us -> 73.2 us (0.85)
  Pallas kernels: 81.1 us -> 71 us
  local copies, waits for them, and re-layouts: 4.62 us -> 1.35 us
    pallas_call x1, Pallas kernels: 81.1 us -> 68.2 us  [shards(): pl.pallas_call(functools.partial(kernel, R, C, S, B, K, g_rows, h_rows),...]
    unnamed x3 -> x1, local copies, waits for them, and re-layouts: 4.62 us -> 1.35 us
    pallas_call x0 -> x1, Pallas kernels: none -> 2.75 us  [shards(): pl.pallas_call(finish, out_shape=(jax.ShapeDtypeStruct((K, T), F32), jax....]
where the time goes in v3:
time: 73.2 us; the launch traced here: 73 us
  Pallas kernels  71 us (97%)
  local copies, waits for them, and re-layouts  1.35 us (2%)
    pallas_call x1, Pallas kernels, shards(): pl.pallas_call(functools.partial(kernel, R, C, S, B, K, g_rows, h_rows),...  68.2 us
    pallas_call x1, Pallas kernels, shards(): pl.pallas_call(finish, out_shape=(jax.ShapeDtypeStruct((K, T), F32), jax....  2.75 us

profile of v3, /device:TPU:0, one launch (start us, length us, event | category | flops | bytes accessed | tf_op | source)
XLA Modules:
  0.0 73.0 jit_solution(8460816407959355058)
XLA Ops:
  0.6 1.4 %copy.7.index_in = s32[5,3]{1,0:T(8,128)} copy(s32[5,3]{0,1:T(4,128)} %param.9) | data formatting | bytes 120 | tf_op args[4]
  2.0 68.2 %shard_map.68 = (f32[64,1024]{1,0:T(8,128)}, f32[5,64,64]{2,1,0:T(8,128)}) custom-call(s32[5,3]{1,0:T(8,128)} %copy.7.index_in, bf16[64,1024]{1,0:T(8,128)(2,1)} %probe_ref.3, bf16[4,64,1024]{2,1,0:T(8,128)(2,1)} %prior_ref.3, f32[1,1024]{1,0:T(1,128)} %bitcast.1, bf16[5,1024,1024]{2,1,0:T(8,128)(2,1)} %tiles_ref.1), custom_call_target="tpu_custom_call" | custom-call | flops 1342177280 | bytes 10485760 | tf_op jit(solution)/shard_map/pallas_call | solution.py:473
  70.2 2.7 %shard_map.69 = (f32[64,1024]{1,0:T(8,128)}, f32[5,64,64]{2,1,0:T(8,128)}) custom-call(f32[64,1024]{1,0:T(8,128)} %get-tuple-element.4.product_ref, f32[5,64,64]{2,1,0:T(8,128)} %get-tuple-element.5.coef_ref, bf16[4,64,1024]{2,1,0:T(8,128)(2,1)} %prior_ref.3, bf16[64,1024]{1,0:T(8,128)(2,1)} %probe_ref.3), custom_call_target="tpu_custom_call" | custom-call | tf_op jit(solution)/shard_map/pallas_call | solution.py:488

commit v4 on v3

--- a/solution.py
+++ b/solution.py
@@ -65,7 +65,7 @@
     index_ref, tile_buf, basis, rowp, colp, fwd, mir, row_part, sib_in, z_sum, z_send, z_in, z_send_scale, z_in_scale,
     col_send, col_in, col_send_scale, col_in_scale,
     g_buf, g1, g2, g2_in, g3, g4, h_buf, h1, h2, h3, aug, solver,
-    index_sem, tile_sem, gz_s, gz_r, gs_s, gs_r, gr_s, gr_r, sb_s, sb_r, zz_s, zz_r, zs_s, zs_r, cc_s, cc_r, cs_s, cs_r,
+    index_sem, prior_sem, tile_sem, gz_s, gz_r, gs_s, gs_r, gr_s, gr_r, sb_s, sb_r, zz_s, zz_r, zs_s, zs_r, cc_s, cc_r, cs_s, cs_r,
     red_row_s, red_row_r, red_col_s, red_col_r, al_row_s, al_row_r, al_col_s, al_col_r,
 ):
     Z = C // 2
@@ -91,6 +91,11 @@
 
     index_copy = pltpu.make_async_copy(index_in, index_ref, index_sem)
     index_copy.start()
+    prior_copies = [
+        pltpu.make_async_copy(prior_ref.at[b], basis.at[pl.ds(b * K, K)], prior_sem.at[b]) for b in range(B - 1)
+    ]
+    for copy in prior_copies:
+        copy.start()
     loop(S, lambda s: local(s).start())
 
     barrier = pltpu.get_barrier_semaphore()
@@ -209,22 +214,27 @@
         peer = (r + 1 + k) % R
         remote(h2.at[peer], h2.at[peer], al_row_s.at[peer], al_row_r.at[peer], peer, c).wait_recv()
 
-    def reduce_along():
+    def along_parts():
         loop(C - 1, lambda k: a1(k).start())
 
+    def along_sums():
         def add(k, total):
             got_a_col(0, h1, k)
             return total + h1[(c + 1 + k) % C]
 
         h2[r] = lax.fori_loop(0, C - 1, add, h_buf[pl.ds(pl.multiple_of(c * h_rows, 8), h_rows), :])
         loop(R - 1, lambda k: a2(k).start())
+
+    def along_totals():
         loop(R - 1, got_a_row)
         h3[c] = lax.fori_loop(1, R, lambda k, total: total + h2[k], h2[0])
         loop(C - 1, lambda k: a3(k).start())
+
+    def along_done():
         loop(C - 1, lambda k: got_a_col(1, h3, k))
 
-    for b in range(B - 1):
-        basis[b * K : (b + 1) * K, :] = prior_ref[b]
+    for copy in prior_copies:
+        copy.wait()
     basis[(B - 1) * K :, :] = probe_ref[...]
     half = K // 2
     used = len(pairs) * half
@@ -251,26 +261,18 @@
 
     def forward(s):
         local(s).wait()
-        right = colp[index_ref[s, 1] // C]
+        right = colp[index_ref[1, s] // C]
         fwd[s] = lax.dot_general(tile_buf[s], right, NT, preferred_element_type=F32).T
 
     loop(S, forward)
-
-    def share_probe(k):
-        peer = (z + 1 + k) % Z
-        slot = peer * 2 + core
-        remote(rowp.at[slot], rowp.at[slot], gz_s.at[peer], gz_r.at[peer], r, slot).wait_recv()
-        sib_gather(peer).start()
-
-    loop(Z - 1, share_probe)
     gram[1]()
 
     def pick(dst, parts, column, number, divide):
         hits = []
         for slot in range(S):
-            value = index_ref[slot, column]
+            value = index_ref[column, slot]
             place = value // C if divide else value % C
-            hits.append(jnp.logical_and(place == number, index_ref[slot, 2] > 0))
+            hits.append(jnp.logical_and(place == number, index_ref[2, slot] > 0))
 
         def some(k):
             rows = pl.ds(pl.multiple_of(k * 16, 16), 16)
@@ -291,6 +293,15 @@
 
     loop(Z, give_sib)
 
+    def share_probe(k):
+        peer = (z + 1 + k) % Z
+        slot = peer * 2 + core
+        remote(rowp.at[slot], rowp.at[slot], gz_s.at[peer], gz_r.at[peer], r, slot).wait_recv()
+        sib_gather(peer).start()
+
+    loop(Z - 1, share_probe)
+    gram[2]()
+
     def to_z(zz):
         return remote(z_send.at[zz], z_in.at[z], zz_s.at[zz], zz_r.at[z], r, zz * 2 + core)
 
@@ -309,35 +320,10 @@
         to_z_scale(zz).start()
 
     loop(Z - 1, give_z)
-    gram[2]()
+    gram[3]()
 
     loop(Z, lambda zz: sib_arrival(zz).wait_recv())
 
-    def mirror(s):
-        left = rowp[index_ref[s, 0] % C]
-        mir[s] = jnp.dot(left, tile_buf[s], preferred_element_type=F32)
-
-    loop(S, mirror)
-
-    gram[3]()
-
-    def to_row(peer):
-        return remote(col_send.at[peer], col_in.at[r], cc_s.at[peer], cc_r.at[r], peer, c)
-
-    def to_row_scale(peer):
-        return remote(col_send_scale.at[peer], col_in_scale.at[r], cs_s.at[peer], cs_r.at[r], peer, c)
-
-    def give_row(k):
-        peer = (r + 1 + k) % R
-        pick(z_sum, mir, 1, peer, True)
-        col_send[peer], col_send_scale[peer] = code(z_sum[...])
-        to_row(peer).start()
-        to_row_scale(peer).start()
-
-    loop(R - 1, give_row)
-    out_ref[...] = self_ref[...] * probe_ref[...].astype(F32) + chip_sum(z)
-    pick(z_sum, mir, 1, r, True)
-    out_ref[...] += z_sum[...]
     gram[4]()
 
     sums = g4[...].reshape(-1, 2 * K)
@@ -365,20 +351,52 @@
         scaled = row / pivot
         aug[...] = jnp.where(all_down == k, scaled, whole - column * scaled)
 
-    loop(K, eliminate)
-    square = jnp.where(lane_of((K, K)) == lax.broadcasted_iota(jnp.int32, (K, K), 0), 1.0, 0.0)
-    for b in range(B):
-        line = [square]
+    wide = 256
+    pieces = S * (out_ref.shape[1] // wide)
+    steps = 2 if 2 * pieces <= K else K // pieces
+
+    def mirror(i):
+        s = i // (pieces // S)
+        columns = pl.ds(pl.multiple_of(i % (pieces // S) * wide, wide), wide)
+        left = rowp[index_ref[0, s] % C]
+        mir[s, :, columns] = jnp.dot(left, tile_buf[s, :, columns], preferred_element_type=F32)
+        for step in range(steps):
+            eliminate(i * steps + step)
+
+    loop(pieces, mirror)
+
+    def to_row(peer):
+        return remote(col_send.at[peer], col_in.at[r], cc_s.at[peer], cc_r.at[r], peer, c)
+
+    def to_row_scale(peer):
+        return remote(col_send_scale.at[peer], col_in_scale.at[r], cs_s.at[peer], cs_r.at[r], peer, c)
+
+    def give_row(k):
+        peer = (r + 1 + k) % R
+        pick(z_sum, mir, 1, peer, True)
+        col_send[peer], col_send_scale[peer] = code(z_sum[...])
+        to_row(peer).start()
+        to_row_scale(peer).start()
+
+    loop(R - 1, give_row)
+    out_ref[...] = self_ref[...] * probe_ref[...].astype(F32) + chip_sum(z)
+    pick(z_sum, mir, 1, r, True)
+    out_ref[...] += z_sum[...]
+
+    loop(K - steps * pieces, lambda k: eliminate(steps * pieces + k))
+
+    inverse = [pltpu.roll(aug[b], K, 1)[:, :K] for b in range(B)]
+
+    def solver_row(b):
+        line = [inverse[b]]
         if b > 0:
             row = jnp.concatenate([gram_blocks[b, a] for a in range(b)], axis=1)
+            scaled = jnp.dot(inverse[b], row, precision=HIGH, preferred_element_type=F32)
             done = solver[: b * K, : b * K]
-            line = [-jnp.dot(row, done, precision=HIGH, preferred_element_type=F32), square]
+            line = [-jnp.dot(scaled, done, precision=HIGH, preferred_element_type=F32), inverse[b]]
         if b < B - 1:
             line.append(jnp.zeros((K, (B - 1 - b) * K), F32))
-        inverse = pltpu.roll(aug[b], K, 1)[:, :K]
-        solver[b * K : (b + 1) * K, :] = jnp.dot(
-            inverse, jnp.concatenate(line, axis=1), precision=HIGH, preferred_element_type=F32
-        )
+        solver[b * K : (b + 1) * K, :] = jnp.concatenate(line, axis=1)
 
     def add_row(k):
         peer = (r + 1 + k) % R
@@ -387,7 +405,6 @@
         remote(lines, lines, cs_s.at[peer], cs_r.at[peer], peer, c).wait_recv()
         out_ref[...] += decode(col_in[peer], col_in_scale[peer])
 
-    loop(R - 1, add_row)
 
     def add_z(k):
         peer = (z + 1 + k) % Z
@@ -397,6 +414,7 @@
         out_ref[...] += decode(z_in[peer], z_in_scale[peer])
 
     loop(Z - 1, add_z)
+    loop(R - 1, add_row)
 
     product = out_ref[...]
     inner = jnp.zeros((B * K, 2 * K), F32)
@@ -405,7 +423,14 @@
         inner = inner + lax.dot_general(basis[...], both, NT, preferred_element_type=F32)
     for b in range(B):
         h_buf[b * half : (b + 1) * half, :] = pack(inner[b * K : (b + 1) * K])
-    reduce_along()
+    along_parts()
+    for b in range(B - 2):
+        solver_row(b)
+    along_sums()
+    solver_row(B - 2)
+    along_totals()
+    solver_row(B - 1)
+    along_done()
     targets = h3[...].reshape(-1, 2 * K)
     stacked = jnp.concatenate([unpack(targets[b * half : (b + 1) * half]) for b in range(B)], axis=0)
     solved = jnp.dot(solver[...], stacked, precision=HIGH, preferred_element_type=F32)
@@ -457,7 +482,7 @@
         ]
 
     scratch = [
-        pltpu.SMEM(tile_index.shape, jnp.int32), vmem((S, T, T), BF16), vmem((B * K, T), BF16), vmem((C, K, T), BF16), vmem((R, K, T), BF16),
+        pltpu.SMEM(tile_index.shape[::-1], jnp.int32), vmem((S, T, T), BF16), vmem((B * K, T), BF16), vmem((C, K, T), BF16), vmem((R, K, T), BF16),
         vmem((S, K, T)), vmem((S, K, T)),
         vmem((Z, K, T)), vmem((Z, K, T)), vmem((K, T)),
         vmem((Z, K, T), I16), vmem((Z, K, T), I16), vmem((Z, 8, 128)), vmem((Z, 8, 128)),
@@ -465,16 +490,17 @@
         *reduce_scratch(g_rows),
         vmem((C * h_rows, W)), vmem((C, h_rows, W)), vmem((R, h_rows, W)), vmem((C, h_rows, W)),
         vmem((B, K, W)), vmem((B * K, B * K)),
-        pltpu.SemaphoreType.DMA, dma(S), dma(Z), dma(Z), dma(Z), dma(Z), dma(R), dma(R), dma(Z), dma(Z),
+        pltpu.SemaphoreType.DMA, dma(B - 1), dma(S), dma(Z), dma(Z), dma(Z), dma(Z), dma(R), dma(R), dma(Z), dma(Z),
         dma(Z), dma(Z), dma(Z), dma(Z), dma(R), dma(R), dma(R), dma(R),
         dma(2, R), dma(2, R), dma(2, C), dma(2, C), dma(R), dma(R), dma(2, C), dma(2, C),
     ]
     in_vmem = pl.BlockSpec(memory_space=pltpu.VMEM)
+    in_any = pl.BlockSpec(memory_space=pl.ANY)
     product, coefficients = pl.pallas_call(
         functools.partial(kernel, R, C, S, B, K, g_rows, h_rows),
         out_shape=(jax.ShapeDtypeStruct((K, T), F32), jax.ShapeDtypeStruct((B, K, K), F32)),
         in_specs=[
-            pl.BlockSpec(memory_space=pl.ANY), in_vmem, in_vmem, in_vmem, pl.BlockSpec(memory_space=pl.ANY),
+            in_any, in_vmem, in_any, in_vmem, in_any,
         ],
         out_specs=(in_vmem, in_vmem),
         scratch_shapes=scratch,
@@ -484,7 +510,7 @@
         cost_estimate=pl.CostEstimate(
             flops=4 * S * K * T * T, bytes_accessed=2 * S * T * T, transcendentals=0
         ),
-    )(tile_index, probe_block, prior_blocks, self_relatedness[None], tile_values)
+    )(tile_index.T, probe_block, prior_blocks, self_relatedness[None], tile_values)
     return pl.pallas_call(
         finish,
         out_shape=(jax.ShapeDtypeStruct((K, T), F32), jax.ShapeDtypeStruct((B, K, K), F32)),

time: 73.2 us -> 64.7 us (0.88)
  Pallas kernels: 71 us -> 63.9 us
  local copies, waits for them, and re-layouts: 1.35 us -> 0 us
    pallas_call x1, Pallas kernels: 68.2 us -> 61.2 us  [shards(): pl.pallas_call(functools.partial(kernel, R, C, S, B, K, g_rows, h_rows),...]
    unnamed x1 -> x0, local copies, waits for them, and re-layouts: 1.35 us -> none
where the time goes in v4:
time: 64.7 us; the launch traced here: 64.5 us
  Pallas kernels  63.9 us (99%)
    pallas_call x1, Pallas kernels, shards(): pl.pallas_call(functools.partial(kernel, R, C, S, B, K, g_rows, h_rows),...  61.2 us
    pallas_call x1, Pallas kernels, shards(): pl.pallas_call(finish, out_shape=(jax.ShapeDtypeStruct((K, T), F32), jax....  2.75 us

profile of v4, /device:TPU:0, one launch (start us, length us, event | category | flops | bytes accessed | tf_op | source)
XLA Modules:
  0.0 64.5 jit_solution(14920351697112061415)
XLA Ops:
  0.6 61.2 %shard_map.68 = (f32[64,1024]{1,0:T(8,128)}, f32[5,64,64]{2,1,0:T(8,128)}) custom-call(s32[3,5]{1,0:T(4,128)} %bitcast.3, bf16[64,1024]{1,0:T(8,128)(2,1)} %probe_ref.3, bf16[4,64,1024]{2,1,0:T(8,128)(2,1)} %prior_ref.3, f32[1,1024]{1,0:T(1,128)} %bitcast.2, bf16[5,1024,1024]{2,1,0:T(8,128)(2,1)} %tiles_ref.1), custom_call_target="tpu_custom_call" | custom-call | flops 1342177280 | bytes 10485760 | tf_op jit(solution)/shard_map/pallas_call | solution.py:499
  61.8 2.7 %shard_map.69 = (f32[64,1024]{1,0:T(8,128)}, f32[5,64,64]{2,1,0:T(8,128)}) custom-call(f32[64,1024]{1,0:T(8,128)} %get-tuple-element.4.product_ref, f32[5,64,64]{2,1,0:T(8,128)} %get-tuple-element.5.coef_ref, bf16[4,64,1024]{2,1,0:T(8,128)(2,1)} %prior_ref.3, bf16[64,1024]{1,0:T(8,128)(2,1)} %probe_ref.3), custom_call_target="tpu_custom_call" | custom-call | tf_op jit(solution)/shard_map/pallas_call | solution.py:514

commit v5 on v4

--- a/solution.py
+++ b/solution.py
@@ -351,39 +351,49 @@
         scaled = row / pivot
         aug[...] = jnp.where(all_down == k, scaled, whole - column * scaled)
 
-    wide = 256
-    pieces = S * (out_ref.shape[1] // wide)
-    steps = 2 if 2 * pieces <= K else K // pieces
-
-    def mirror(i):
-        s = i // (pieces // S)
-        columns = pl.ds(pl.multiple_of(i % (pieces // S) * wide, wide), wide)
-        left = rowp[index_ref[0, s] % C]
-        mir[s, :, columns] = jnp.dot(left, tile_buf[s, :, columns], preferred_element_type=F32)
-        for step in range(steps):
-            eliminate(i * steps + step)
-
-    loop(pieces, mirror)
-
-    def to_row(peer):
-        return remote(col_send.at[peer], col_in.at[r], cc_s.at[peer], cc_r.at[r], peer, c)
-
-    def to_row_scale(peer):
-        return remote(col_send_scale.at[peer], col_in_scale.at[r], cs_s.at[peer], cs_r.at[r], peer, c)
-
-    def give_row(k):
-        peer = (r + 1 + k) % R
-        pick(z_sum, mir, 1, peer, True)
-        col_send[peer], col_send_scale[peer] = code(z_sum[...])
-        to_row(peer).start()
-        to_row_scale(peer).start()
-
-    loop(R - 1, give_row)
+    Q, wide = col_send.shape[1], col_send.shape[3]
+    given = 2 if Q * (2 * S + 2 * (R - 1)) <= K else 0
+    per_chunk = 2 * S + given * (R - 1)
+
+    def to_row(peer, q):
+        return remote(col_send.at[peer, q], col_in.at[r, q], cc_s.at[peer, q], cc_r.at[r, q], peer, c)
+
+    def to_row_scale(peer, q):
+        return remote(
+            col_send_scale.at[peer, q], col_in_scale.at[r, q], cs_s.at[peer, q], cs_r.at[r, q], peer, c
+        )
+
+    def chunk(q):
+        columns = pl.ds(pl.multiple_of(q * wide, wide), wide)
+
+        def mirror(s):
+            left = rowp[index_ref[0, s] % C]
+            mir[s, :, columns] = jnp.dot(left, tile_buf[s, :, columns], preferred_element_type=F32)
+            for step in range(2):
+                eliminate(q * per_chunk + 2 * s + step)
+
+        loop(S, mirror)
+
+        def give_row(k):
+            peer = (r + 1 + k) % R
+            total = jnp.zeros((K, wide), F32)
+            for slot in range(S):
+                hit = jnp.logical_and(index_ref[1, slot] // C == peer, index_ref[2, slot] > 0)
+                total = total + jnp.where(hit, mir[slot, :, columns], 0.0)
+            col_send[peer, q], col_send_scale[peer, q] = code(total)
+            to_row(peer, q).start()
+            to_row_scale(peer, q).start()
+            for step in range(given):
+                eliminate(q * per_chunk + 2 * S + given * k + step)
+
+        loop(R - 1, give_row)
+
+    loop(Q, chunk)
     out_ref[...] = self_ref[...] * probe_ref[...].astype(F32) + chip_sum(z)
     pick(z_sum, mir, 1, r, True)
     out_ref[...] += z_sum[...]
 
-    loop(K - steps * pieces, lambda k: eliminate(steps * pieces + k))
+    loop(K - Q * per_chunk, lambda k: eliminate(Q * per_chunk + k))
 
     inverse = [pltpu.roll(aug[b], K, 1)[:, :K] for b in range(B)]
 
@@ -398,13 +408,17 @@
             line.append(jnp.zeros((K, (B - 1 - b) * K), F32))
         solver[b * K : (b + 1) * K, :] = jnp.concatenate(line, axis=1)
 
-    def add_row(k):
+    solver_row(0)
+    solver_row(1)
+
+    def add_row(i):
+        q, k = i // (R - 1), i % (R - 1)
         peer = (r + 1 + k) % R
-        remote(col_in.at[peer], col_in.at[peer], cc_s.at[peer], cc_r.at[peer], peer, c).wait_recv()
-        lines = col_in_scale.at[peer]
-        remote(lines, lines, cs_s.at[peer], cs_r.at[peer], peer, c).wait_recv()
-        out_ref[...] += decode(col_in[peer], col_in_scale[peer])
-
+        values, lines = col_in.at[peer, q], col_in_scale.at[peer, q]
+        remote(values, values, cc_s.at[peer, q], cc_r.at[peer, q], peer, c).wait_recv()
+        remote(lines, lines, cs_s.at[peer, q], cs_r.at[peer, q], peer, c).wait_recv()
+        columns = pl.ds(pl.multiple_of(q * wide, wide), wide)
+        out_ref[:, columns] += decode(col_in[peer, q], col_in_scale[peer, q])
 
     def add_z(k):
         peer = (z + 1 + k) % Z
@@ -414,17 +428,17 @@
         out_ref[...] += decode(z_in[peer], z_in_scale[peer])
 
     loop(Z - 1, add_z)
-    loop(R - 1, add_row)
+    loop(Q * (R - 1), add_row)
 
     product = out_ref[...]
-    inner = jnp.zeros((B * K, 2 * K), F32)
-    for part in split3(product)[::-1]:
-        both = jnp.concatenate([part, part], axis=0)
-        inner = inner + lax.dot_general(basis[...], both, NT, preferred_element_type=F32)
+    hi, mid, lo = split3(product)
+    parts = jnp.concatenate([lo, lo, mid, mid, hi, hi], axis=0)
+    inner = lax.dot_general(basis[...], parts, NT, preferred_element_type=F32)
+    inner = inner[:, : 2 * K] + inner[:, 2 * K : 4 * K] + inner[:, 4 * K :]
     for b in range(B):
         h_buf[b * half : (b + 1) * half, :] = pack(inner[b * K : (b + 1) * K])
     along_parts()
-    for b in range(B - 2):
+    for b in range(2, B - 2):
         solver_row(b)
     along_sums()
     solver_row(B - 2)
@@ -446,8 +460,13 @@
     loop(Z, lambda zz: to_sib(zz).wait_send())
     loop(Z - 1, lambda k: to_z((z + 1 + k) % Z).wait_send())
     loop(Z - 1, lambda k: to_z_scale((z + 1 + k) % Z).wait_send())
-    loop(R - 1, lambda k: to_row((r + 1 + k) % R).wait_send())
-    loop(R - 1, lambda k: to_row_scale((r + 1 + k) % R).wait_send())
+
+    def row_left(i):
+        q, k = i // (R - 1), i % (R - 1)
+        to_row((r + 1 + k) % R, q).wait_send()
+        to_row_scale((r + 1 + k) % R, q).wait_send()
+
+    loop(Q * (R - 1), row_left)
 
 
 def finish(product_ref, coef_ref, prior_ref, probe_ref, out_ref, coef_out):
@@ -455,11 +474,10 @@
     coef_out[...] = coef_ref[...]
     stacked = coef_ref[...].reshape(B * K, K)
     last = (B - 1) * K
-    taken = jnp.zeros(out_ref.shape, F32)
-    for part in split3(stacked.T)[::-1]:
-        for b in range(B - 1):
-            taken = taken + jnp.dot(part[:, b * K : (b + 1) * K], prior_ref[b], preferred_element_type=F32)
-        taken = taken + jnp.dot(part[:, last:], probe_ref[...], preferred_element_type=F32)
+    parts = jnp.concatenate(split3(stacked.T)[::-1], axis=0)
+    taken = jnp.dot(parts[:, :last], prior_ref[...].reshape(last, -1), preferred_element_type=F32)
+    taken = taken + jnp.dot(parts[:, last:], probe_ref[...], preferred_element_type=F32)
+    taken = taken[:K] + taken[K : 2 * K] + taken[2 * K :]
     out_ref[...] = product_ref[...] - taken
 
 
@@ -474,6 +492,7 @@
     vmem = lambda shape, dtype=F32: pltpu.VMEM(shape, dtype)
     dma = lambda *shape: pltpu.SemaphoreType.DMA(shape)
     W = 2 * K
+    Q = T // 256
 
     def reduce_scratch(rows):
         return [
@@ -486,12 +505,12 @@
         vmem((S, K, T)), vmem((S, K, T)),
         vmem((Z, K, T)), vmem((Z, K, T)), vmem((K, T)),
         vmem((Z, K, T), I16), vmem((Z, K, T), I16), vmem((Z, 8, 128)), vmem((Z, 8, 128)),
-        vmem((R, K, T), I16), vmem((R, K, T), I16), vmem((R, 8, 128)), vmem((R, 8, 128)),
+        vmem((R, Q, K, T // Q), I16), vmem((R, Q, K, T // Q), I16), vmem((R, Q, 8, 128)), vmem((R, Q, 8, 128)),
         *reduce_scratch(g_rows),
         vmem((C * h_rows, W)), vmem((C, h_rows, W)), vmem((R, h_rows, W)), vmem((C, h_rows, W)),
         vmem((B, K, W)), vmem((B * K, B * K)),
         pltpu.SemaphoreType.DMA, dma(B - 1), dma(S), dma(Z), dma(Z), dma(Z), dma(Z), dma(R), dma(R), dma(Z), dma(Z),
-        dma(Z), dma(Z), dma(Z), dma(Z), dma(R), dma(R), dma(R), dma(R),
+        dma(Z), dma(Z), dma(Z), dma(Z), dma(R, Q), dma(R, Q), dma(R, Q), dma(R, Q),
         dma(2, R), dma(2, R), dma(2, C), dma(2, C), dma(R), dma(R), dma(2, C), dma(2, C),
     ]
     in_vmem = pl.BlockSpec(memory_space=pltpu.VMEM)

time: 64.7 us -> 65.2 us (level)
    pallas_call x1, Pallas kernels: 61.2 us -> 62.1 us  [shards(): pl.pallas_call(functools.partial(kernel, R, C, S, B, K, g_rows, h_rows),...]
where the time goes in v5:
time: 65.2 us; the launch traced here: 65.1 us
  Pallas kernels  64.4 us (99%)
    pallas_call x1, Pallas kernels, shards(): pl.pallas_call(functools.partial(kernel, R, C, S, B, K, g_rows, h_rows),...  62.1 us
    pallas_call x1, Pallas kernels, shards(): pl.pallas_call(finish, out_shape=(jax.ShapeDtypeStruct((K, T), F32), jax....  2.34 us

profile of v5, /device:TPU:0, one launch (start us, length us, event | category | flops | bytes accessed | tf_op | source)
XLA Modules:
  0.0 65.1 jit_solution(13836382804552296643)
XLA Ops:
  0.6 62.1 %shard_map.68 = (f32[64,1024]{1,0:T(8,128)}, f32[5,64,64]{2,1,0:T(8,128)}) custom-call(s32[3,5]{1,0:T(4,128)} %bitcast.3, bf16[64,1024]{1,0:T(8,128)(2,1)} %probe_ref.3, bf16[4,64,1024]{2,1,0:T(8,128)(2,1)} %prior_ref.3, f32[1,1024]{1,0:T(1,128)} %bitcast.2, bf16[5,1024,1024]{2,1,0:T(8,128)(2,1)} %tiles_ref.1), custom_call_target="tpu_custom_call" | custom-call | flops 1342177280 | bytes 10485760 | tf_op jit(solution)/shard_map/pallas_call | solution.py:518
  62.7 2.3 %shard_map.69 = (f32[64,1024]{1,0:T(8,128)}, f32[5,64,64]{2,1,0:T(8,128)}) custom-call(f32[64,1024]{1,0:T(8,128)} %get-tuple-element.4.product_ref, f32[5,64,64]{2,1,0:T(8,128)} %get-tuple-element.5.coef_ref, bf16[4,64,1024]{2,1,0:T(8,128)(2,1)} %prior_ref.3, bf16[64,1024]{1,0:T(8,128)(2,1)} %probe_ref.3), custom_call_target="tpu_custom_call" | custom-call | tf_op jit(solution)/shard_map/pallas_call | solution.py:533

commit v6 on v5

--- a/solution.py
+++ b/solution.py
@@ -344,16 +344,27 @@
     row_lanes = lane_of((B, 1, 2 * K))
 
     def eliminate(k):
+        one, two = 2 * k, 2 * k + 1
         whole = aug[...]
-        row = aug[:, pl.ds(k, 1), :]
-        column = jnp.sum(jnp.where(all_lanes == k, whole, 0.0), axis=2, keepdims=True)
-        pivot = jnp.sum(jnp.where(row_lanes == k, row, 0.0), axis=2, keepdims=True)
-        scaled = row / pivot
-        aug[...] = jnp.where(all_down == k, scaled, whole - column * scaled)
+        row1, row2 = aug[:, pl.ds(one, 1), :], aug[:, pl.ds(two, 1), :]
+
+        def at(values, where, number):
+            return jnp.sum(jnp.where(where == number, values, 0.0), axis=2, keepdims=True)
+
+        column1, column2 = at(whole, all_lanes, one), at(whole, all_lanes, two)
+        p11, p12 = at(row1, row_lanes, one), at(row1, row_lanes, two)
+        p21, p22 = at(row2, row_lanes, one), at(row2, row_lanes, two)
+        first = 1.0 / p11
+        ratio = p21 * first
+        second = 1.0 / (p22 - p12 * ratio)
+        scaled2 = (row2 - ratio * row1) * second
+        scaled1 = (row1 - p12 * scaled2) * first
+        rest = whole - column1 * scaled1 - column2 * scaled2
+        aug[...] = jnp.where(all_down == one, scaled1, jnp.where(all_down == two, scaled2, rest))
 
     Q, wide = col_send.shape[1], col_send.shape[3]
-    given = 2 if Q * (2 * S + 2 * (R - 1)) <= K else 0
-    per_chunk = 2 * S + given * (R - 1)
+    given = 1 if Q * (S + R - 1) <= K // 2 else 0
+    per_chunk = S + given * (R - 1)
 
     def to_row(peer, q):
         return remote(col_send.at[peer, q], col_in.at[r, q], cc_s.at[peer, q], cc_r.at[r, q], peer, c)
@@ -369,8 +380,7 @@
         def mirror(s):
             left = rowp[index_ref[0, s] % C]
             mir[s, :, columns] = jnp.dot(left, tile_buf[s, :, columns], preferred_element_type=F32)
-            for step in range(2):
-                eliminate(q * per_chunk + 2 * s + step)
+            eliminate(q * per_chunk + s)
 
         loop(S, mirror)
 
@@ -383,8 +393,8 @@
             col_send[peer, q], col_send_scale[peer, q] = code(total)
             to_row(peer, q).start()
             to_row_scale(peer, q).start()
-            for step in range(given):
-                eliminate(q * per_chunk + 2 * S + given * k + step)
+            if given:
+                eliminate(q * per_chunk + S + k)
 
         loop(R - 1, give_row)
 
@@ -393,7 +403,7 @@
     pick(z_sum, mir, 1, r, True)
     out_ref[...] += z_sum[...]
 
-    loop(K - Q * per_chunk, lambda k: eliminate(Q * per_chunk + k))
+    loop(K // 2 - Q * per_chunk, lambda k: eliminate(Q * per_chunk + k))
 
     inverse = [pltpu.roll(aug[b], K, 1)[:, :K] for b in range(B)]
 
@@ -492,7 +502,7 @@
     vmem = lambda shape, dtype=F32: pltpu.VMEM(shape, dtype)
     dma = lambda *shape: pltpu.SemaphoreType.DMA(shape)
     W = 2 * K
-    Q = T // 256
+    Q = T // 512
 
     def reduce_scratch(rows):
         return [

time: 65.2 us -> 61.9 us (0.949)
  Pallas kernels: 64.4 us -> 61.1 us
    pallas_call x1, Pallas kernels: 62.1 us -> 58.8 us  [shards(): pl.pallas_call(functools.partial(kernel, R, C, S, B, K, g_rows, h_rows),...]
where the time goes in v6:
time: 61.9 us; the launch traced here: 61.8 us
  Pallas kernels  61.1 us (99%)
  between operations  0.64 us (1%)
    pallas_call x1, Pallas kernels, shards(): pl.pallas_call(functools.partial(kernel, R, C, S, B, K, g_rows, h_rows),...  58.8 us
    pallas_call x1, Pallas kernels, shards(): pl.pallas_call(finish, out_shape=(jax.ShapeDtypeStruct((K, T), F32), jax....  2.34 us

profile of v6, /device:TPU:0, one launch (start us, length us, event | category | flops | bytes accessed | tf_op | source)
XLA Modules:
  0.0 61.8 jit_solution(12534024906578595526)
XLA Ops:
  0.6 58.8 %shard_map.68 = (f32[64,1024]{1,0:T(8,128)}, f32[5,64,64]{2,1,0:T(8,128)}) custom-call(s32[3,5]{1,0:T(4,128)} %bitcast.3, bf16[64,1024]{1,0:T(8,128)(2,1)} %probe_ref.3, bf16[4,64,1024]{2,1,0:T(8,128)(2,1)} %prior_ref.3, f32[1,1024]{1,0:T(1,128)} %bitcast.2, bf16[5,1024,1024]{2,1,0:T(8,128)(2,1)} %tiles_ref.1), custom_call_target="tpu_custom_call" | custom-call | flops 1342177280 | bytes 10485760 | tf_op jit(solution)/shard_map/pallas_call | solution.py:528
  59.4 2.3 %shard_map.69 = (f32[64,1024]{1,0:T(8,128)}, f32[5,64,64]{2,1,0:T(8,128)}) custom-call(f32[64,1024]{1,0:T(8,128)} %get-tuple-element.4.product_ref, f32[5,64,64]{2,1,0:T(8,128)} %get-tuple-element.5.coef_ref, bf16[4,64,1024]{2,1,0:T(8,128)(2,1)} %prior_ref.3, bf16[64,1024]{1,0:T(8,128)(2,1)} %probe_ref.3), custom_call_target="tpu_custom_call" | custom-call | tf_op jit(solution)/shard_map/pallas_call | solution.py:543

commit v7 on v6

--- a/solution.py
+++ b/solution.py
@@ -324,6 +324,48 @@
 
     loop(Z, lambda zz: sib_arrival(zz).wait_recv())
 
+    Q, wide = col_send.shape[1], col_send.shape[3]
+    per_body = K // 2 // (2 * S)
+    given = 2 if 2 * (R - 1) + per_body * S <= K // 2 else 0
+    shared = per_body * S + given * (R - 1)
+
+    def to_row(peer, q):
+        return remote(col_send.at[peer, q], col_in.at[r, q], cc_s.at[peer, q], cc_r.at[r, q], peer, c)
+
+    def to_row_scale(peer, q):
+        return remote(
+            col_send_scale.at[peer, q], col_in_scale.at[r, q], cs_s.at[peer, q], cs_r.at[r, q], peer, c
+        )
+
+    def chunk(q, step=None):
+        columns = pl.ds(q * wide, wide)
+
+        def mirror(s):
+            left = rowp[index_ref[0, s] % C]
+            mir[s, :, columns] = jnp.dot(left, tile_buf[s, :, columns], preferred_element_type=F32)
+            if step is not None:
+                for i in range(per_body):
+                    step(per_body * s + i)
+
+        loop(S, mirror)
+
+        def give_row(k):
+            peer = (r + 1 + k) % R
+            total = jnp.zeros((K, wide), F32)
+            for slot in range(S):
+                hit = jnp.logical_and(index_ref[1, slot] // C == peer, index_ref[2, slot] > 0)
+                total = total + jnp.where(hit, mir[slot, :, columns], 0.0)
+            col_send[peer, q], col_send_scale[peer, q] = code(total)
+            to_row(peer, q).start()
+            to_row_scale(peer, q).start()
+            if step is not None:
+                for i in range(given):
+                    step(per_body * S + given * k + i)
+
+        loop(R - 1, give_row)
+
+    for q in range(Q - 1):
+        chunk(q)
     gram[4]()
 
     sums = g4[...].reshape(-1, 2 * K)
@@ -362,48 +404,12 @@
         rest = whole - column1 * scaled1 - column2 * scaled2
         aug[...] = jnp.where(all_down == one, scaled1, jnp.where(all_down == two, scaled2, rest))
 
-    Q, wide = col_send.shape[1], col_send.shape[3]
-    given = 1 if Q * (S + R - 1) <= K // 2 else 0
-    per_chunk = S + given * (R - 1)
-
-    def to_row(peer, q):
-        return remote(col_send.at[peer, q], col_in.at[r, q], cc_s.at[peer, q], cc_r.at[r, q], peer, c)
-
-    def to_row_scale(peer, q):
-        return remote(
-            col_send_scale.at[peer, q], col_in_scale.at[r, q], cs_s.at[peer, q], cs_r.at[r, q], peer, c
-        )
-
-    def chunk(q):
-        columns = pl.ds(pl.multiple_of(q * wide, wide), wide)
-
-        def mirror(s):
-            left = rowp[index_ref[0, s] % C]
-            mir[s, :, columns] = jnp.dot(left, tile_buf[s, :, columns], preferred_element_type=F32)
-            eliminate(q * per_chunk + s)
-
-        loop(S, mirror)
-
-        def give_row(k):
-            peer = (r + 1 + k) % R
-            total = jnp.zeros((K, wide), F32)
-            for slot in range(S):
-                hit = jnp.logical_and(index_ref[1, slot] // C == peer, index_ref[2, slot] > 0)
-                total = total + jnp.where(hit, mir[slot, :, columns], 0.0)
-            col_send[peer, q], col_send_scale[peer, q] = code(total)
-            to_row(peer, q).start()
-            to_row_scale(peer, q).start()
-            if given:
-                eliminate(q * per_chunk + S + k)
-
-        loop(R - 1, give_row)
-
-    loop(Q, chunk)
+    chunk(Q - 1, eliminate)
     out_ref[...] = self_ref[...] * probe_ref[...].astype(F32) + chip_sum(z)
     pick(z_sum, mir, 1, r, True)
     out_ref[...] += z_sum[...]
 
-    loop(K // 2 - Q * per_chunk, lambda k: eliminate(Q * per_chunk + k))
+    loop(K // 2 - shared, lambda k: eliminate(shared + k))
 
     inverse = [pltpu.roll(aug[b], K, 1)[:, :K] for b in range(B)]
 

time: 61.9 us -> 60.9 us (0.984)
  Pallas kernels: 61.1 us -> 60.1 us
    pallas_call x1, Pallas kernels: 58.8 us -> 57.8 us  [shards(): pl.pallas_call(functools.partial(kernel, R, C, S, B, K, g_rows, h_rows),...]
where the time goes in v7:
time: 60.9 us; the launch traced here: 60.7 us
  Pallas kernels  60.1 us (99%)
  between operations  0.64 us (1%)
    pallas_call x1, Pallas kernels, shards(): pl.pallas_call(functools.partial(kernel, R, C, S, B, K, g_rows, h_rows),...  57.8 us
    pallas_call x1, Pallas kernels, shards(): pl.pallas_call(finish, out_shape=(jax.ShapeDtypeStruct((K, T), F32), jax....  2.34 us

profile of v7, /device:TPU:0, one launch (start us, length us, event | category | flops | bytes accessed | tf_op | source)
XLA Modules:
  0.0 60.7 jit_solution(16850822304182301100)
XLA Ops:
  0.6 57.8 %shard_map.68 = (f32[64,1024]{1,0:T(8,128)}, f32[5,64,64]{2,1,0:T(8,128)}) custom-call(s32[3,5]{1,0:T(4,128)} %bitcast.3, bf16[64,1024]{1,0:T(8,128)(2,1)} %probe_ref.3, bf16[4,64,1024]{2,1,0:T(8,128)(2,1)} %prior_ref.3, f32[1,1024]{1,0:T(1,128)} %bitcast.2, bf16[5,1024,1024]{2,1,0:T(8,128)(2,1)} %tiles_ref.1), custom_call_target="tpu_custom_call" | custom-call | flops 1342177280 | bytes 10485760 | tf_op jit(solution)/shard_map/pallas_call | solution.py:534
  58.4 2.3 %shard_map.69 = (f32[64,1024]{1,0:T(8,128)}, f32[5,64,64]{2,1,0:T(8,128)}) custom-call(f32[64,1024]{1,0:T(8,128)} %get-tuple-element.4.product_ref, f32[5,64,64]{2,1,0:T(8,128)} %get-tuple-element.5.coef_ref, bf16[4,64,1024]{2,1,0:T(8,128)(2,1)} %prior_ref.3, bf16[64,1024]{1,0:T(8,128)(2,1)} %probe_ref.3), custom_call_target="tpu_custom_call" | custom-call | tf_op jit(solution)/shard_map/pallas_call | solution.py:549
